TPU v7x, 256 devices: a whole 4x4x8 slice. The times are simulated.
256 devices in a mesh: gx: 16 (over z, x_hi), gy: 16 (over y, x_lo, core).
Axes of the slice: x: 4 (x_hi: 2, x_lo: 2; x = x_hi * 2 + x_lo), y: 4, z: 8, core: 2. Of those that a mesh axis runs over, the one named last changes fastest.
Arguments:
- saturation: bfloat16 [20, 256, 256, 256], P(None, 'gx', 'gy'), may hold values from -6 to 6
- spectral_weight: float32 [2, 768, 24, 20, 20], P(None, ('gx', 'gy')), may hold values from -18 to 18
- pointwise_weight: bfloat16 [20, 20], replicated, may hold values from -1.25 to 1.25
- pointwise_bias: float32 [20], replicated, may hold values from -3 to 3
- cotangent: bfloat16 [20, 256, 256, 256], P(None, 'gx', 'gy'), may hold values from -6 to 6
Outputs:
- layer_output: bfloat16 [20, 256, 256, 256], P(None, 'gx', 'gy')
- input_gradient: bfloat16 [20, 256, 256, 256], P(None, 'gx', 'gy')
- spectral_gradient: float32 [2, 768, 24, 20, 20], P(None, ('gx', 'gy'))
All inputs are finite; a program needn't handle non-finite values.
Results may differ from a plain program's by a relative error of at most 0.038.
Values may be sent and summed in bfloat16 or wider, within the bound.
No kernel may reach another device: no remote copies, remote signals or barrier semaphores. Data moves between devices by JAX's collectives and lax.ppermute only.
A program may use at most 128 MiB of HBM per device.

v0:
```python
import math

import jax
import jax.numpy as jnp
from jax import lax
from jax.sharding import PartitionSpec as P

C = 20
Z = 32
T_SIZE = 8
KX = 24
KY = 24
KZ = 8
KT = 4
M = 32


highest = lax.Precision.HIGHEST


def kept_frequency(kept_count):
    position = jnp.arange(kept_count, dtype=jnp.int32)
    return jnp.where(position < kept_count // 2, position, position - kept_count)


def axis_table(length, kept_count, offset, row_total):
    positions = offset + jnp.arange(row_total, dtype=jnp.int32)
    product = positions[:, None] * kept_frequency(kept_count)[None, :] % length
    phase_angle = product.astype(jnp.float32) * (2.0 * math.pi / length)
    cosine = jnp.cos(phase_angle) * (1.0 / math.sqrt(length))
    sine_part = jnp.sin(phase_angle) * (1.0 / math.sqrt(length))
    real_rows = jnp.stack([cosine, -sine_part], axis=-1)
    imag_rows = jnp.stack([sine_part, cosine], axis=-1)
    return jnp.stack([real_rows, imag_rows], axis=1).astype(jnp.bfloat16)


def depth_time_table():
    cell_index = jnp.arange(Z * T_SIZE, dtype=jnp.int32)
    depth_index = cell_index // T_SIZE
    time_index = cell_index % T_SIZE
    depth_part = (depth_index[:, None] * kept_frequency(KZ)[None, :] % Z).astype(jnp.float32) * (
        1.0 / Z
    )
    time_part = (time_index[:, None] * jnp.arange(KT, dtype=jnp.int32)[None, :] % T_SIZE).astype(
        jnp.float32
    ) * (1.0 / T_SIZE)
    phase_angle = (depth_part[:, :, None] + time_part[:, None, :]).reshape(Z * T_SIZE, KZ * KT) * (
        2.0 * math.pi
    )
    norm_scale = 1.0 / math.sqrt(Z * T_SIZE)
    return jnp.stack(
        [jnp.cos(phase_angle) * norm_scale, -jnp.sin(phase_angle) * norm_scale], axis=-1
    ).astype(jnp.bfloat16)


def gelu_value(pre_value):
    return 0.5 * pre_value * (1.0 + lax.erf(pre_value * (1.0 / math.sqrt(2.0))))


def gelu_slope(pre_value):
    return 0.5 * (1.0 + lax.erf(pre_value * (1.0 / math.sqrt(2.0)))) + pre_value * jnp.exp(
        -0.5 * pre_value * pre_value
    ) * (1.0 / math.sqrt(2.0 * math.pi))


def mix(spectrum, weight_real, weight_imag):
    real_part = spectrum[:, :, 0, :]
    imag_part = spectrum[:, :, 1, :]
    out_real = jnp.einsum("slio,sli->slo", weight_real, real_part, precision=highest) - jnp.einsum(
        "slio,sli->slo", weight_imag, imag_part, precision=highest
    )
    out_imag = jnp.einsum("slio,sli->slo", weight_real, imag_part, precision=highest) + jnp.einsum(
        "slio,sli->slo", weight_imag, real_part, precision=highest
    )
    return jnp.stack([out_real, out_imag], axis=2)


def outer_gradient(spectrum, upstream):
    real_part = spectrum[:, :, 0, :]
    imag_part = spectrum[:, :, 1, :]
    upstream_real = upstream[:, :, 0, :]
    upstream_imag = upstream[:, :, 1, :]
    real_gradient = jnp.einsum(
        "slo,sli->slio", upstream_real, real_part, precision=highest
    ) + jnp.einsum("slo,sli->slio", upstream_imag, imag_part, precision=highest)
    imag_gradient = jnp.einsum(
        "slo,sli->slio", upstream_imag, real_part, precision=highest
    ) - jnp.einsum("slo,sli->slio", upstream_real, imag_part, precision=highest)
    return jnp.stack([real_gradient, imag_gradient], axis=0)


def back_mix(upstream, weight_real, weight_imag):
    upstream_real = upstream[:, :, 0, :]
    upstream_imag = upstream[:, :, 1, :]
    into_real = jnp.einsum(
        "slio,slo->sli", weight_real, upstream_real, precision=highest
    ) + jnp.einsum("slio,slo->sli", weight_imag, upstream_imag, precision=highest)
    into_imag = jnp.einsum(
        "slio,slo->sli", weight_real, upstream_imag, precision=highest
    ) - jnp.einsum("slio,slo->sli", weight_imag, upstream_real, precision=highest)
    return jnp.stack([into_real, into_imag], axis=2)


def item_factor(item_total):
    block_index = lax.axis_index("gx") * lax.axis_size("gy") + lax.axis_index("gy")
    item_index = block_index * item_total + jnp.arange(item_total, dtype=jnp.int32)
    return jnp.where(item_index // KX % KT == 0, 1.0, 2.0).astype(jnp.float32)


def analyse(volume, depth_table):
    rows_here = volume.shape[1]
    columns_here = volume.shape[2]
    gx_count = lax.axis_size("gx")
    per_device = M // gx_count
    depth_modes = jnp.einsum(
        "cxyz,zmr->xmcyr", volume, depth_table, preferred_element_type=jnp.float32
    ).astype(jnp.bfloat16)
    row_table = axis_table(rows_here * gx_count, KX, lax.axis_index("gx") * rows_here, rows_here)
    partial_term = jnp.einsum(
        "xmcyr,xrkq->mkqcy", depth_modes, row_table, preferred_element_type=jnp.float32
    )
    summed = lax.psum_scatter(
        partial_term.reshape(per_device * lax.axis_size("gx"), KX * 2 * C * columns_here).astype(
            jnp.bfloat16
        ),
        "gx",
        scatter_dimension=0,
        tiled=True,
    )
    row_modes = summed.reshape(per_device, KX, 2, C, columns_here)
    item_rows = row_modes.reshape(per_device * KX, 2 * C, columns_here)
    spread = lax.all_to_all(item_rows, "gy", split_axis=0, concat_axis=2, tiled=True)
    whole_columns = spread.shape[2]
    spread = spread.reshape(spread.shape[0], 2, C, whole_columns)
    column_table = axis_table(whole_columns, KY, 0, whole_columns)
    return jnp.einsum("srcy,yrlq->slqc", spread, column_table, preferred_element_type=jnp.float32)


def synthesise(mode_array, depth_table, rows_here, columns_here):
    gx_count = lax.axis_size("gx")
    whole_columns = columns_here * lax.axis_size("gy")
    column_table = axis_table(whole_columns, KY, 0, whole_columns).astype(jnp.float32)
    column_part = jnp.einsum("slqc,yrlq->srcy", mode_array, column_table, precision=highest).astype(
        jnp.bfloat16
    )
    returned = lax.all_to_all(
        column_part.reshape(mode_array.shape[0], 2 * C, whole_columns),
        "gy",
        split_axis=2,
        concat_axis=0,
        tiled=True,
    )
    per_device = returned.shape[0] // KX
    row_table = axis_table(rows_here * gx_count, KX, lax.axis_index("gx") * rows_here, rows_here)
    gathered = lax.all_gather(
        returned.reshape(per_device, KX * 2 * C * columns_here), "gx", axis=0, tiled=True
    )
    mode_count = gathered.shape[0]
    mode_grid = gathered.reshape(mode_count, KX, 2, C, columns_here)
    row_part = jnp.einsum(
        "mkqcy,xrkq->xmcyr", mode_grid, row_table, preferred_element_type=jnp.float32
    ).astype(jnp.bfloat16)
    rows_local = row_part.reshape(rows_here, mode_count, C * columns_here * 2)
    rows_local = rows_local.reshape(rows_here, M, C, columns_here, 2)
    return jnp.einsum(
        "xmcyr,zmr->cxyz", rows_local, depth_table, preferred_element_type=jnp.float32
    )


def shards(saturation, spectral_weight, pointwise_weight, pointwise_bias, cotangent):
    rows_here = saturation.shape[1]
    columns_here = saturation.shape[2]
    depth_table = depth_time_table()
    weight_real = spectral_weight[0]
    weight_imag = spectral_weight[1]
    spectrum = analyse(saturation, depth_table)
    factor = item_factor(spectrum.shape[0])[:, None, None, None]
    mixed_modes = mix(spectrum, weight_real, weight_imag) * factor
    spectral = synthesise(mixed_modes, depth_table, rows_here, columns_here)
    bias_column = pointwise_bias[:, None, None, None]
    preactivation = (
        spectral
        + jnp.einsum(
            "io,ixyz->oxyz", pointwise_weight, saturation, preferred_element_type=jnp.float32
        )
        + bias_column
    )
    layer_output = gelu_value(preactivation).astype(jnp.bfloat16)
    slope_field = (cotangent.astype(jnp.float32) * gelu_slope(preactivation)).astype(jnp.bfloat16)
    upstream = analyse(slope_field, depth_table) * factor
    spectral_gradient = outer_gradient(spectrum, upstream)
    returned = back_mix(upstream, weight_real, weight_imag)
    input_spectral = synthesise(returned, depth_table, rows_here, columns_here)
    input_gradient = (
        input_spectral
        + jnp.einsum(
            "io,oxyz->ixyz", pointwise_weight, slope_field, preferred_element_type=jnp.float32
        )
    ).astype(jnp.bfloat16)
    return (layer_output, input_gradient, spectral_gradient)


def solution(mesh):
    return jax.shard_map(
        shards,
        mesh=mesh,
        in_specs=(
            P(None, "gx", "gy", None),
            P(None, ("gx", "gy"), None, None, None),
            P(),
            P(),
            P(None, "gx", "gy", None),
        ),
        out_specs=(
            P(None, "gx", "gy", None),
            P(None, "gx", "gy", None),
            P(None, ("gx", "gy"), None, None, None),
        ),
        check_vma=False,
    )
```

profile of v0, /device:TPU:1, one launch (start us, length us, event | category | flops | bytes accessed | tf_op | source)
XLA Modules:
  0.0 675.0 jit_solution(8063209734663968532)
XLA Ops:
  8.9 3.6 fusion.8
  12.5 4.9 copy.55
  20.2 3.5 fusion.111
  23.7 191.6 %all-reduce.5.cloned.1.call-done = bf16[32,15360]{0,1:T(8,128)(2,1)} async-done(((bf16[32,15360]{0,1:T(8,128)(2,1)}), bf16[32,15360]{0,1:T(8,128)(2,1)}) %all-reduce.5.cloned.1.call-update) | async-done | bytes 983056
  215.3 4.0 constant_dynamic-slice_fusion.1
  219.3 3.5 copy.56
  226.1 9.5 %all-to-all-start = ((bf16[16,2,960]{2,1,0:T(2,128)(2,1)}), bf16[16,2,960]{2,1,0:T(2,128)(2,1)S(1)}, u32[]{:S(2)}, u32[]{:S(2)}) async-start(bf16[16,2,960]{2,1,0:T(2,128)(2,1)} %reshape.609), calls=%async_computation | async-start | bytes 131072 | tf_op jit(solution)/shard_map/all_to_all | solution.py:132
  236.2 5.2 all-to-all-done
  250.6 10.3 %all_to_all.60 = bf16[16,2,960]{2,1,0:T(2,128)(2,1)} all-to-all(bf16[16,2,960]{2,1,0:T(2,128)(2,1)} %reshape.611), channel_id=1, replica_groups=mesh['gx'=16,'gy'=16] {'gy'}, dimensions={0} | all-to-all | bytes 122880 | tf_op jit(solution)/shard_map/all_to_all | solution.py:146
  262.8 1.9 copy.65
  266.3 40.3 %all-gather = bf16[16,2,15360]{2,1,0:T(2,128)(2,1)} all-gather(bf16[1,2,15360]{2,1,0:T(2,128)(2,1)S(1)} %reshape.548), channel_id=1, replica_groups=mesh['gx'=16,'gy'=16] {'gx'}, dimensions={0}, use_global_device_ids=true | all-gather | bytes 1044480 | tf_op jit(solution)/shard_map/all_gather | solution.py:155
  306.6 11.0 %reshape.540 = bf16[32,24,2,20,16]{4,3,2,1,0:T(8,128)(2,1)} reshape(bf16[16,2,15360]{2,1,0:T(2,128)(2,1)} %all-gather) | data formatting | bytes 1966080 | tf_op jit(solution)/shard_map/reshape | solution.py:159
  317.6 15.9 %copy.67 = bf16[32,24,2,20,16]{0,1,2,4,3:T(8,128)(2,1)} copy(bf16[32,24,2,20,16]{4,3,2,1,0:T(8,128)(2,1)} %reshape.540) | data formatting | bytes 1966080 | tf_op jit(solution)/shard_map/reshape | solution.py:159
  333.4 3.0 fusion.22
  336.5 3.3 fusion.18
  339.8 7.6 %fusion.5 = (bf16[20,16,16,256]{3,0,2,1:T(8,128)(2,1)}, bf16[20,16,16,256]{3,0,2,1:T(8,128)(2,1)}) fusion(bf16[20,16,16,256]{3,2,1,0:T(8,128)(2,1)S(1)} %copy-done.18, f32[20]{0:T(128)S(1)} %copy-done.19, bf16[20,16,16,256]{3,2,1,0:T(8,128)(2,1)S(1)} %copy-done, bf16[20,20]{1,0:T(8,128)(2,1)S(1)} %copy-done.15, f32[256,16,20,16,1]{0,2,4,3,1:T(8,128)S(1)} %fusion.18), kind=kOutput, calls=%fused_computation.8 | convolution fusion | flops 73400320 | bytes 15729520 | tf_op jit(solution)/shard_map/io,ixyz->oxyz/dot_general | solution.py:183
  347.3 7.1 %fusion.9 = bf16[32,24,2,20,16]{0,1,4,3,2:T(8,128)(2,1)} fusion(bf16[20,16,16,256,1]{3,0,2,1,4:T(8,128)(2,1)} %bitcast.275, bf16[16,1,24,2]{2,0,1,3:T(8,128)(2,1)S(1)} %copy-done.13, bf16[16,1,24,2]{2,0,1,3:T(8,128)(2,1)S(1)} %copy-done.10, bf16[256,32,1]{0,1,2:T(8,128)(2,1)S(1)} %reshape.547, bf16[256,32,1]{0,1,2:T(8,128)(2,1)S(1)} %mul.417), kind=kOutput, calls=%fused_computation.18 | convolution fusion | flops 200120320 | bytes 3640320 | tf_op jit(solution)/shard_map/xmcyr,xrkq->mkqcy/dot_general | solution.py:119
  354.4 4.9 copy.73
  359.3 195.8 %all-reduce.7.cloned.1.call-done = bf16[32,15360]{0,1:T(8,128)(2,1)} async-done(((bf16[32,15360]{0,1:T(8,128)(2,1)}), bf16[32,15360]{0,1:T(8,128)(2,1)}) %all-reduce.7.cloned.1.call-update) | async-done | bytes 983056
  555.2 4.0 constant_dynamic-slice_fusion
  559.2 3.7 copy.74
  564.4 9.6 %all-to-all-start.2 = ((bf16[16,2,960]{2,1,0:T(2,128)(2,1)}), bf16[16,2,960]{2,1,0:T(2,128)(2,1)S(1)}, u32[]{:S(2)}, u32[]{:S(2)}) async-start(bf16[16,2,960]{2,1,0:T(2,128)(2,1)} %reshape.613), calls=%async_computation.2 | async-start | bytes 131072 | tf_op jit(solution)/shard_map/all_to_all | solution.py:132
  574.0 4.0 copy.89
  583.7 3.9 all-to-all-start.3
  587.7 2.0 copy.91
  589.7 3.7 all-to-all-done.3
  594.6 37.9 %all-gather.1 = bf16[16,2,15360]{2,1,0:T(2,128)(2,1)S(1)} all-gather(bf16[1,2,15360]{2,1,0:T(2,128)(2,1)S(1)} %reshape.550), channel_id=1, replica_groups=mesh['gx'=16,'gy'=16] {'gx'}, dimensions={0}, use_global_device_ids=true | all-gather | bytes 1044480 | tf_op jit(solution)/shard_map/all_gather | solution.py:155
  632.6 9.9 %reshape.544 = bf16[32,24,2,20,16]{4,3,2,1,0:T(8,128)(2,1)} reshape(bf16[16,2,15360]{2,1,0:T(2,128)(2,1)S(1)} %all-gather.1) | data formatting | bytes 1966080 | tf_op jit(solution)/shard_map/reshape | solution.py:159
  642.4 15.9 %copy.83 = bf16[32,24,2,20,16]{0,1,2,4,3:T(8,128)(2,1)} copy(bf16[32,24,2,20,16]{4,3,2,1,0:T(8,128)(2,1)} %reshape.544) | data formatting | bytes 1966080 | tf_op jit(solution)/shard_map/reshape | solution.py:159
  658.3 3.0 fusion.23
  661.3 3.3 fusion.14
  665.9 2.1 copy.90
  (108 shorter events, 29.8 us)
Async XLA Ops:
  7.2 1.7 copy-start
  7.2 208.1 %all-reduce.5.cloned.1.call-start = ((), (), s32[]{:S(2)}) async-start(), calls=%async_computation.4 | async-start | bytes 7864320
  8.9 8.5 %copy-start.9 = (bf16[16,1,24,2]{2,0,1,3:T(8,128)(2,1)}, bf16[16,1,24,2]{2,0,1,3:T(8,128)(2,1)S(1)}, u32[]{:S(2)}) copy-start(bf16[16,1,24,2]{2,0,1,3:T(8,128)(2,1)S(1)} %get-tuple-element.38) | copy-start | bytes 4612
  8.9 8.5 %copy-start.12 = (bf16[16,1,24,2]{2,0,1,3:T(8,128)(2,1)}, bf16[16,1,24,2]{2,0,1,3:T(8,128)(2,1)S(1)}, u32[]{:S(2)}) copy-start(bf16[16,1,24,2]{2,0,1,3:T(8,128)(2,1)S(1)} %get-tuple-element.39) | copy-start | bytes 4612
  17.4 0.7 copy-start.20
  226.1 15.3 %all-to-all-start = ((bf16[16,2,960]{2,1,0:T(2,128)(2,1)}), bf16[16,2,960]{2,1,0:T(2,128)(2,1)S(1)}, u32[]{:S(2)}, u32[]{:S(2)}) async-start(bf16[16,2,960]{2,1,0:T(2,128)(2,1)} %reshape.609), calls=%async_computation | async-start | bytes 131072 | tf_op jit(solution)/shard_map/all_to_all | solution.py:132
  235.6 319.6 %all-reduce.7.cloned.1.call-start = ((), (), s32[]{:S(2)}) async-start(), calls=%async_computation.5 | async-start | bytes 7864320
  245.3 2.7 copy-start.4
  245.4 2.6 copy-start.6
  317.5 15.9 %copy-start.10 = (bf16[16,1,24,2]{2,0,1,3:T(8,128)(2,1)S(1)}, bf16[16,1,24,2]{2,0,1,3:T(8,128)(2,1)}, u32[]{:S(2)}) copy-start(bf16[16,1,24,2]{2,0,1,3:T(8,128)(2,1)} %copy-done.9) | copy-start | bytes 4612
  317.6 15.9 %copy-start.13 = (bf16[16,1,24,2]{2,0,1,3:T(8,128)(2,1)S(1)}, bf16[16,1,24,2]{2,0,1,3:T(8,128)(2,1)}, u32[]{:S(2)}) copy-start(bf16[16,1,24,2]{2,0,1,3:T(8,128)(2,1)} %copy-done.12) | copy-start | bytes 4612
  336.4 3.3 copy-start.15
  336.5 3.3 copy-start.18
  336.5 3.3 copy-start.19
  563.5 17.4 %copy-start.8 = (bf16[256,1,24,2]{0,2,1,3:T(8,128)(2,1)S(1)}, bf16[256,1,24,2]{0,2,1,3:T(8,128)(2,1)}, u32[]{:S(2)}) copy-start(bf16[256,1,24,2]{0,2,1,3:T(8,128)(2,1)} %get-tuple-element.35) | copy-start | bytes 73732
  563.5 17.4 %copy-start.17 = (f32[3]{0:T(128)S(1)}, f32[3]{0:T(128)}, u32[]{:S(2)}) copy-start(f32[3]{0:T(128)} %compare_select_fusion.4) | copy-start | bytes 40
  564.4 17.0 %copy-start.3 = (f32[1,3,24,20,20]{2,0,4,3,1:T(1,128)S(1)}, f32[1,3,24,20,20]{2,0,4,3,1:T(1,128)}, u32[]{:S(2)}) copy-start(f32[1,3,24,20,20]{2,0,4,3,1:T(1,128)} %get-tuple-element.27) | copy-start | bytes 345604
  564.4 15.4 %all-to-all-start.2 = ((bf16[16,2,960]{2,1,0:T(2,128)(2,1)}), bf16[16,2,960]{2,1,0:T(2,128)(2,1)S(1)}, u32[]{:S(2)}, u32[]{:S(2)}) async-start(bf16[16,2,960]{2,1,0:T(2,128)(2,1)} %reshape.613), calls=%async_computation.2 | async-start | bytes 131072 | tf_op jit(solution)/shard_map/all_to_all | solution.py:132
  574.0 8.0 %copy-start.5 = (f32[3,24,20]{1,2,0:T(8,128)S(1)}, f32[3,24,20]{1,2,0:T(8,128)}, u32[]{:S(2)}) copy-start(f32[3,24,20]{1,2,0:T(8,128)} %copy-done.4) | copy-start | bytes 17284
  574.0 8.0 %copy-start.7 = (f32[3,24,20]{1,2,0:T(8,128)S(1)}, f32[3,24,20]{1,2,0:T(8,128)}, u32[]{:S(2)}) copy-start(f32[3,24,20]{1,2,0:T(8,128)} %copy-done.6) | copy-start | bytes 17284
  583.7 9.7 %all-to-all-start.3 = ((bf16[16,2,960]{2,1,0:T(2,128)(2,1)}), bf16[16,2,960]{2,1,0:T(2,128)(2,1)S(1)}, u32[]{:S(2)}, u32[]{:S(2)}) async-start(bf16[16,2,960]{2,1,0:T(2,128)(2,1)} %reshape.615), calls=%async_computation.3 | async-start | bytes 131072 | tf_op jit(solution)/shard_map/all_to_all | solution.py:146
  642.4 15.9 %copy-start.11 = (bf16[16,1,24,2]{2,0,1,3:T(8,128)(2,1)S(1)}, bf16[16,1,24,2]{2,0,1,3:T(8,128)(2,1)}, u32[]{:S(2)}) copy-start(bf16[16,1,24,2]{2,0,1,3:T(8,128)(2,1)} %copy-done.9) | copy-start | bytes 4612
  642.4 15.9 %copy-start.14 = (bf16[16,1,24,2]{2,0,1,3:T(8,128)(2,1)S(1)}, bf16[16,1,24,2]{2,0,1,3:T(8,128)(2,1)}, u32[]{:S(2)}) copy-start(bf16[16,1,24,2]{2,0,1,3:T(8,128)(2,1)} %copy-done.12) | copy-start | bytes 4612
  661.3 3.3 copy-start.2
  661.3 3.3 copy-start.16
  664.6 3.3 copy-start.1
Sparse Core Ops, SparseCore 0:
  17.6 197.6 all-reduce.4
  359.5 195.6 all-reduce.6
where the time goes:
time: 688 us; the launch traced here: 675 us
  waiting for transfers between devices  398 us (58%)
  local copies, waits for them, and re-layouts  111 us (16%)
  blocking collectives  88.5 us (13%)
  matrix products  34.4 us (5%)
  starting transfers between devices  23.1 us (3%)
  between operations  15.4 us (2%)
    unnamed x4, waiting for transfers between devices  387 us
    all_gather x2, blocking collectives, synthesise(): lax.all_gather(returned.reshape(per_device, KX * 2 * C * columns_here), '...  78.2 us
    reshape x4, local copies, waits for them, and re-layouts, synthesise(): mode_grid = gathered.reshape(mode_count, KX, 2, C, columns_here)  52.6 us
    unnamed x62, local copies, waits for them, and re-layouts  26.6 us
    all_to_all x2, starting transfers between devices, analyse(): lax.all_to_all(item_rows, 'gy', split_axis=0, concat_axis=2, tiled=True)  19.1 us
  transfers between devices with their start and end apart: 5, of which 5 were waited for; matrix products, arithmetic and copies ran while one was open for 2% of the time, Pallas kernels for 0%

commit v1 on v0

v1 whole, which is shorter than its diff:
```python
import functools
import math

import jax
import jax.numpy as jnp
import numpy as np
from jax import lax
from jax.experimental import pallas as pl
from jax.experimental.pallas import tpu as pltpu
from jax.sharding import PartitionSpec as P

C = 20
Z = 32
T_SIZE = 8
L = 256
K = 24
KZ = 8
KT = 4
M = 32
G = 16
CY = C * G
VMEM = 48 * 1024 * 1024
BF = jnp.bfloat16
F32 = jnp.float32


def kept_frequency(kept_count):
    position = np.arange(kept_count)
    return np.where(position < kept_count // 2, position, position - kept_count)


def axis_table():
    product = (np.arange(L)[:, None] * kept_frequency(K)[None, :]) % L
    angle = product.astype(np.float32) * np.float32(2.0 * math.pi / L)
    cosine = np.cos(angle) * np.float32(1.0 / math.sqrt(L))
    sine = np.sin(angle) * np.float32(1.0 / math.sqrt(L))
    return np.stack([np.stack([cosine, -sine], -1), np.stack([sine, cosine], -1)], 1)


def depth_table():
    cell = np.arange(Z * T_SIZE)
    depth = ((cell // T_SIZE)[:, None] * kept_frequency(KZ)[None, :] % Z).astype(np.float32) / np.float32(Z)
    time = ((cell % T_SIZE)[:, None] * np.arange(KT)[None, :] % T_SIZE).astype(np.float32) / np.float32(T_SIZE)
    angle = (depth[:, :, None] + time[:, None, :]).reshape(Z * T_SIZE, M) * np.float32(2.0 * math.pi)
    scale = np.float32(1.0 / math.sqrt(Z * T_SIZE))
    table = np.stack([np.cos(angle) * scale, -np.sin(angle) * scale], -1)
    return table.reshape(Z * T_SIZE, 2 * M).T


def row_matrix():
    table = axis_table().reshape(G, 4, 2, 2, 2, 8, 3, 2)
    out = np.zeros((2, 2, 8, 8, G, 4, 2, 2, 2), np.float32)
    part = table.transpose(2, 5, 6, 7, 0, 1, 3, 4).reshape(2, 8, 6, G, 4, 2, 2)
    for pair in range(2):
        out[:, pair, :, :6, :, :, :, pair, :] = part
    return out.reshape(256, 512)


def column_matrix():
    table = axis_table().reshape(G, G, 2, K, 2)
    out = np.zeros((G, G, 8, 2, 128), np.float32)
    for t in range(3):
        for r in range(2):
            out[:, :, 2 * t + r, :, t * K : (t + 1) * K] = table[:, :, r].transpose(1, 0, 3, 2)
    return out.reshape(2048, 256)


def order_matrix():
    out = np.zeros((G, 32, C, G), np.float32)
    for y in range(G):
        for c in range(C):
            out[y, c, c, y] = 1.0
    return out.reshape(512, CY)


def dot(a, b, contract=(1, 0)):
    return lax.dot_general(
        a, b, (((contract[0],), (contract[1],)), ((), ())), preferred_element_type=F32
    )


def pack(first, second):
    first = first.reshape(8, 8, 2 * CY)
    second = second.reshape(8, 8, 2 * CY)
    low = lax.broadcasted_iota(jnp.int32, first.shape, 1) < 4
    even = jnp.where(low, first, pltpu.roll(second, 4, 1))
    odd = jnp.where(low, pltpu.roll(first, 4, 1), second)
    return even, odd


def send_planes(plane, depth, send_ref):
    evens, odds = [], []
    for g in range(2):
        parts = []
        for e in range(2):
            planes = jnp.concatenate([plane(4 * g + e), plane(4 * g + 2 + e)], 0)
            parts.append(dot(depth, planes, (1, 1)))
        even, odd = pack(*parts)
        evens.append(even)
        odds.append(odd)
    send_ref[:, 0] = jnp.concatenate(evens, 1).astype(BF)
    send_ref[:, 1] = jnp.concatenate(odds, 1).astype(BF)


def synthesis(received_ref, g, e, depth):
    rows = received_ref[...].astype(F32)
    even = rows[:, 0, 8 * g : 8 * g + 8]
    odd = rows[:, 1, 8 * g : 8 * g + 8]
    low = lax.broadcasted_iota(jnp.int32, even.shape, 1) < 4
    if e == 0:
        both = jnp.where(low, even, pltpu.roll(odd, 4, 1))
    else:
        both = jnp.where(low, pltpu.roll(even, 4, 1), odd)
    return dot(both.reshape(64, 2 * CY).astype(BF), depth, (0, 0))


def depth_kernel(volume_ref, depth_ref, send_ref):
    send_planes(lambda x: volume_ref[:, x].reshape(CY, L), depth_ref[...], send_ref)


def row_kernel(received_ref, matrix_ref, send_ref):
    product = dot(matrix_ref[...], received_ref[...].reshape(512, 2 * CY))
    total = product[:128] + pltpu.roll(product[128:], CY, 1)
    send_ref[...] = total[:, :CY].reshape(G, 8, CY).astype(BF)


def row_back_kernel(received_ref, matrix_ref, send_ref):
    modes = received_ref[...].astype(F32).reshape(128, CY)
    zeros = jnp.zeros((128, CY), F32)
    upper = jnp.concatenate([modes, zeros], 1)
    lower = jnp.concatenate([zeros, modes], 1)
    both = jnp.concatenate([upper, lower], 0).astype(BF)
    send_ref[...] = dot(matrix_ref[...], both).reshape(G, 32, 2 * CY).astype(BF)


def column_analysis(received_ref, order_ref, column_ref):
    rows = dot(order_ref[...], received_ref[...].reshape(128, CY), (1, 1))
    lanes = jnp.concatenate([rows[32 * y : 32 * y + 32] for y in range(G)], 1)
    return dot(lanes.astype(BF), column_ref[...])


def column_synthesis(modes, order_ref, column_ref, send_ref):
    lanes = dot(modes.astype(BF), column_ref[...], (1, 1))
    rows = jnp.concatenate([lanes[:, 128 * y : 128 * y + 128] for y in range(G)], 0)
    send_ref[...] = dot(rows.astype(BF), order_ref[...], (0, 0)).reshape(G, 8, CY).astype(BF)


def mix_kernel(received_ref, order_ref, column_ref, weight_ref, factor_ref, send_ref, spectrum_ref, mixed_ref):
    spectrum_ref[...] = column_analysis(received_ref, order_ref, column_ref)
    factor = factor_ref[0]
    real = jnp.zeros((C, 128), F32)
    imag = jnp.zeros((C, 128), F32)
    for i in range(C):
        spectrum_real = spectrum_ref[i : i + 1, :128]
        spectrum_imag = spectrum_ref[i : i + 1, 128:]
        weight_real = weight_ref[0, i]
        weight_imag = weight_ref[1, i]
        real += weight_real * spectrum_real - weight_imag * spectrum_imag
        imag += weight_real * spectrum_imag + weight_imag * spectrum_real
    mixed_ref[...] = jnp.zeros((32, 256), F32)
    mixed_ref[:C, :128] = real * factor
    mixed_ref[:C, 128:] = imag * factor
    column_synthesis(mixed_ref[...], order_ref, column_ref, send_ref)


def back_mix_kernel(received_ref, order_ref, column_ref, weight_ref, factor_ref, send_ref, upstream_ref, mixed_ref):
    upstream_ref[...] = column_analysis(received_ref, order_ref, column_ref) * factor_ref[0]
    real = upstream_ref[:C, :128]
    imag = upstream_ref[:C, 128:]
    mixed_ref[...] = jnp.zeros((32, 256), F32)
    for i in range(C):
        weight_real = weight_ref[0, i]
        weight_imag = weight_ref[1, i]
        mixed_ref[i : i + 1, :128] = jnp.sum(weight_real * real + weight_imag * imag, 0, keepdims=True)
        mixed_ref[i : i + 1, 128:] = jnp.sum(weight_real * imag - weight_imag * real, 0, keepdims=True)
    column_synthesis(mixed_ref[...], order_ref, column_ref, send_ref)


def gradient_kernel(spectrum_ref, upstream_ref, gradient_ref):
    real = upstream_ref[:C, :128]
    imag = upstream_ref[:C, 128:]
    for i in range(C):
        spectrum_real = spectrum_ref[i : i + 1, :128]
        spectrum_imag = spectrum_ref[i : i + 1, 128:]
        gradient_ref[0, i] = real * spectrum_real + imag * spectrum_imag
        gradient_ref[1, i] = imag * spectrum_real - real * spectrum_imag


def activation(pre):
    half = jnp.abs(pre) * (1.0 / math.sqrt(2.0))
    bell = jnp.exp(-0.5 * pre * pre)
    t = 1.0 / (1.0 + 0.3275911 * half)
    poly = t * (0.254829592 + t * (-0.284496736 + t * (1.421413741 + t * (-1.453152027 + t * 1.061405429))))
    tail = 0.5 * poly * bell
    return jnp.where(pre < 0.0, tail, 1.0 - tail), bell * (1.0 / math.sqrt(2.0 * math.pi))


def forward_kernel(
    received_ref, volume_ref, cotangent_ref, depth_ref, point_ref, bias_ref, output_ref, slope_ref, send_ref, pre_ref
):
    depth = depth_ref[...]
    point = point_ref[...]
    for g in range(2):
        for e in range(2):
            pre_ref[...] = synthesis(received_ref, g, e, depth)
            for h in range(2):
                x = 4 * g + 2 * h + e
                pre_ref[h * CY : (h + 1) * CY] += dot(point, volume_ref[:, x].reshape(CY, L))

                def step(n, carry):
                    for k in range(2):
                        c = n * 2 + k
                        pre = pre_ref[pl.ds(pl.multiple_of(h * CY + c * G, G), G)] + bias_ref[c]
                        cumulative, density = activation(pre)
                        output_ref[c, x] = (pre * cumulative).astype(BF)
                        slope = cotangent_ref[c, x].astype(F32) * (cumulative + pre * density)
                        slope_ref[c, x] = slope.astype(BF)
                    return carry

                lax.fori_loop(0, C // 2, step, 0)
    send_planes(lambda x: slope_ref[:, x].reshape(CY, L), depth, send_ref)


def backward_kernel(received_ref, slope_ref, depth_ref, point_ref, output_ref):
    depth = depth_ref[...]
    point = point_ref[...]
    for g in range(2):
        for e in range(2):
            spectral = synthesis(received_ref, g, e, depth)
            for h in range(2):
                x = 4 * g + 2 * h + e
                total = spectral[h * CY : (h + 1) * CY] + dot(point, slope_ref[:, x].reshape(CY, L))
                output_ref[:, x] = total.reshape(C, G, L).astype(BF)


def whole(shape):
    return pl.BlockSpec(shape, lambda *_: (0,) * len(shape))


SMEM = pl.BlockSpec(memory_space=pltpu.SMEM)
FIELD = jax.ShapeDtypeStruct((C, G, G, L), BF)
PLANES = pl.BlockSpec((C, 8, G, L), lambda n: (0, n, 0, 0))
BIG = jax.ShapeDtypeStruct((8, 2, 32, 2 * CY), BF)
BIG_ROWS = pl.BlockSpec((8, 2, 16, 2 * CY), lambda n: (0, 0, n, 0))
SMALL = jax.ShapeDtypeStruct((G, 8, CY), BF)
MODES = jax.ShapeDtypeStruct((32, 256), F32)


def call(kernel, out_shape, in_specs=None, out_specs=None, grid=(), scratch=(), flops=0, moved=0):
    extra = {}
    if in_specs is not None:
        extra = {"in_specs": in_specs, "out_specs": out_specs}
    return pl.pallas_call(
        kernel,
        out_shape=out_shape,
        grid=grid,
        scratch_shapes=scratch,
        compiler_params=pltpu.CompilerParams(vmem_limit_bytes=VMEM),
        cost_estimate=pl.CostEstimate(flops=int(flops), bytes_accessed=moved, transcendentals=0),
        **extra,
    )


def exchange_rows(packed):
    moved = lax.all_to_all(packed.reshape(G, 32, 2 * CY), "gx", 0, 0, tiled=True)
    return moved


def exchange_columns(packed):
    return lax.all_to_all(packed, "gy", 0, 0, tiled=True)


def shards(saturation, spectral_weight, pointwise_weight, pointwise_bias, cotangent):
    depth = jnp.asarray(depth_table(), BF)
    rows = jnp.asarray(row_matrix(), BF)
    rows_back = jnp.asarray(row_matrix().T, BF)
    columns = jnp.asarray(column_matrix(), BF)
    order = jnp.asarray(order_matrix(), BF)
    eye = jnp.eye(G, dtype=BF)
    point_back = jnp.kron(pointwise_weight, eye)
    point = jnp.kron(pointwise_weight.T, eye)
    pair = lax.axis_index("gx") * 2 + lax.axis_index("gy") // 8
    factor = jnp.where(pair % KT == 0, 1.0, 2.0).astype(F32).reshape(1)
    weight = jnp.transpose(spectral_weight.reshape(2, 3 * K, C, C), (0, 2, 3, 1))
    weight = jnp.pad(weight, ((0, 0), (0, 0), (0, 0), (0, 128 - 3 * K)))

    depth_call = call(
        depth_kernel, BIG, [PLANES, whole((64, L))], BIG_ROWS, (2,), flops=170e6, moved=3300000
    )
    row_call = call(row_kernel, SMALL, flops=170e6, moved=1000000)
    row_back_call = call(row_back_kernel, jax.ShapeDtypeStruct((G, 32, 2 * CY), BF), flops=170e6, moved=1000000)
    mix_scratch = [pltpu.VMEM((32, 256), F32)]
    vm = pl.BlockSpec(memory_space=pltpu.VMEM)
    mix_specs = [vm, vm, vm, vm, SMEM]
    mix_call = call(mix_kernel, (SMALL, MODES), mix_specs, (vm, vm), (), mix_scratch, 200e6, 2500000)
    back_mix_call = call(back_mix_kernel, (SMALL, MODES), mix_specs, (vm, vm), (), mix_scratch, 200e6, 2500000)
    gradient_call = call(gradient_kernel, jax.ShapeDtypeStruct((2, C, C, 128), F32), flops=1e6, moved=1000000)

    received = exchange_rows(depth_call(saturation, depth))
    received = exchange_columns(row_call(received, rows))
    sent, spectrum = mix_call(received, order, columns, weight, factor)
    received = exchange_columns(sent)
    received = exchange_rows(row_back_call(received, rows_back))
    layer_output, slope, sent = call(
        forward_kernel,
        (FIELD, FIELD, BIG),
        [BIG_ROWS, PLANES, PLANES, whole((64, L)), whole((CY, CY)), SMEM],
        (PLANES, PLANES, BIG_ROWS),
        (2,),
        [pltpu.VMEM((2 * CY, L), F32)],
        1500e6,
        12000000,
    )(received.reshape(BIG.shape), saturation, cotangent, depth, point, pointwise_bias)
    received = exchange_rows(sent)
    received = exchange_columns(row_call(received, rows))
    sent, upstream = back_mix_call(received, order, columns, weight, factor)
    gradient = gradient_call(spectrum, upstream)
    received = exchange_columns(sent)
    received = exchange_rows(row_back_call(received, rows_back))
    input_gradient = call(
        backward_kernel,
        FIELD,
        [BIG_ROWS, PLANES, whole((64, L)), whole((CY, CY))],
        PLANES,
        (2,),
        (),
        1300e6,
        6000000,
    )(received.reshape(BIG.shape), slope, depth, point_back)
    gradient = jnp.transpose(gradient[..., : 3 * K], (0, 3, 1, 2)).reshape(2, 3, K, C, C)
    return layer_output, input_gradient, gradient


def solution(mesh):
    return jax.shard_map(
        shards,
        mesh=mesh,
        in_specs=(
            P(None, "gx", "gy", None),
            P(None, ("gx", "gy"), None, None, None),
            P(),
            P(),
            P(None, "gx", "gy", None),
        ),
        out_specs=(
            P(None, "gx", "gy", None),
            P(None, "gx", "gy", None),
            P(None, ("gx", "gy"), None, None, None),
        ),
        check_vma=False,
    )
```

time: 688 us -> 182 us (0.26); the launches traced: 675 us -> 181 us
  waiting for transfers between devices: 398 us -> 29.5 us
  local copies, waits for them, and re-layouts: 111 us -> 17.6 us
  matrix products: 34.4 us -> 0 us
  Pallas kernels: 0 us -> 28.8 us
  between operations: 15.4 us -> 0.81 us
  starting transfers between devices: 23.1 us -> 14.2 us
    unnamed x4 -> x0, waiting for transfers between devices: 387 us -> none
    all_gather x2 -> x0, blocking collectives: 78.2 us -> none  [synthesise(): lax.all_gather(returned.reshape(per_device, KX * 2 * C * columns_here), '...]
    all_to_all x1 -> x5, blocking collectives: 10.3 us -> 87.3 us  [the longest x2 58.1 us: exchange_rows(): lax.all_to_all(packed.reshape(G, 32, 2 * CY), 'gx', 0, 0, tiled=True)]
    reshape x10 -> x3, local copies, waits for them, and re-layouts: 56.4 us -> 5.79 us  [the longest x2 4.01 us: shards(): spectral_weight.reshape(2, 3 * K, C, C)]
    dot_general x12 -> x0, matrix products: 34.4 us -> none  [the longest x2 10.6 us: analyse(): jnp.einsum('xmcyr,xrkq->mkqcy', depth_modes, row_table, preferred_element...]
    pallas_call x0 -> x10, Pallas kernels: none -> 28.8 us  [the longest x1 17.1 us: shards(): call(forward_kernel, (FIELD, FIELD, BIG), [BIG_ROWS, PLANES, PLANES, whol...]
    unnamed x62 -> x31, local copies, waits for them, and re-layouts: 26.6 us -> 7.59 us
    all_to_all x3, waiting for transfers between devices: 10.7 us -> 29.5 us  [the longest x2 27.8 us: exchange_rows(): lax.all_to_all(packed.reshape(G, 32, 2 * CY), 'gx', 0, 0, tiled=True)]
  transfers between devices with their start and end apart: 5 -> 3, of which waited for: 5 -> 3; matrix products, arithmetic and copies ran while one was open for 2% -> 9% of each run, Pallas kernels for 0% -> 0%
where the time goes in v1:
time: 182 us; the launch traced here: 181 us
  blocking collectives  87.3 us (48%)
  waiting for transfers between devices  29.5 us (16%)
  Pallas kernels  28.8 us (16%)
  local copies, waits for them, and re-layouts  17.6 us (10%)
  starting transfers between devices  14.2 us (8%)
  other arithmetic  2.26 us (1%)
    all_to_all x2, blocking collectives, exchange_rows(): lax.all_to_all(packed.reshape(G, 32, 2 * CY), 'gx', 0, 0, tiled=True)  58.1 us
    all_to_all x3, blocking collectives, exchange_columns(): return lax.all_to_all(packed, 'gy', 0, 0, tiled=True)  29.2 us
    all_to_all x2, waiting for transfers between devices, exchange_rows(): lax.all_to_all(packed.reshape(G, 32, 2 * CY), 'gx', 0, 0, tiled=True)  27.8 us
    pallas_call x1, Pallas kernels, shards(): call(forward_kernel, (FIELD, FIELD, BIG), [BIG_ROWS, PLANES, PLANES, whol...  17.1 us
    unnamed x31, local copies, waits for them, and re-layouts  7.59 us
    all_to_all x2, starting transfers between devices, exchange_rows(): lax.all_to_all(packed.reshape(G, 32, 2 * CY), 'gx', 0, 0, tiled=True)  7.5 us
    all_to_all x1, starting transfers between devices, exchange_columns(): return lax.all_to_all(packed, 'gy', 0, 0, tiled=True)  6.75 us
    reshape x2, local copies, waits for them, and re-layouts, shards(): spectral_weight.reshape(2, 3 * K, C, C)  4.01 us
  transfers between devices with their start and end apart: 3, of which 3 were waited for; matrix products, arithmetic and copies ran while one was open for 9% of the time, Pallas kernels for 0%

profile of v1, /device:TPU:1, one launch (start us, length us, event | category | flops | bytes accessed | tf_op | source)
XLA Modules:
  0.0 180.6 jit_solution(8944735511883110533)
XLA Ops:
  0.6 1.7 copy-done
  2.4 0.8 copy-done.7
  3.1 1.3 shard_map.121
  4.4 32.6 %all_to_all.40.received_ref = bf16[16,32,640]{2,1,0:T(8,128)(2,1)S(1)} all-to-all(bf16[16,32,640]{2,1,0:T(8,128)(2,1)S(1)} %bitcast.15), channel_id=1, replica_groups=mesh['gx'=16,'gy'=16] {'gx'}, dimensions={0} | all-to-all | bytes 1310720 | tf_op jit(solution)/shard_map/all_to_all | solution.py:265
  37.0 1.1 shard_map.122
  38.1 6.7 %all-to-all-start.1 = ((bf16[16,8,320]{2,1,0:T(8,128)(2,1)}), bf16[16,8,320]{2,1,0:T(8,128)(2,1)S(1)}, u32[]{:S(2)}, u32[]{:S(2)}) async-start(bf16[16,8,320]{2,1,0:T(8,128)(2,1)} %shard_map.122), calls=%async_computation.1 | async-start | bytes 196608 | tf_op jit(solution)/shard_map/all_to_all | solution.py:270
  44.9 2.0 %copy.21 = f32[2,3,24,20,20]{2,1,4,3,0:T(4,128)} copy(f32[2,3,24,20,20]{2,0,4,3,1:T(2,128)S(1)} %copy-done.13) | data formatting | bytes 460800 | tf_op jit(solution)/shard_map/reshape | solution.py:284
  46.9 2.0 %reshape.53 = f32[2,72,20,20]{1,3,2,0:T(8,128)S(1)} reshape(f32[2,3,24,20,20]{2,1,4,3,0:T(4,128)} %copy.21) | data formatting | bytes 460800 | tf_op jit(solution)/shard_map/reshape | solution.py:284
  48.9 1.8 all-to-all-done.1.received_ref
  50.7 1.3 shard_map.123
  52.0 9.6 %all_to_all.41.received_ref = bf16[16,8,320]{2,1,0:T(8,128)(2,1)S(1)} all-to-all(bf16[16,8,320]{2,1,0:T(8,128)(2,1)S(1)} %get-tuple-element.10), channel_id=1, replica_groups=mesh['gx'=16,'gy'=16] {'gy'}, dimensions={0} | all-to-all | bytes 163840 | tf_op jit(solution)/shard_map/all_to_all | solution.py:270
  61.7 1.2 shard_map.124
  62.9 3.6 %all-to-all-start.3 = ((bf16[16,32,640]{2,1,0:T(8,128)(2,1)}), bf16[16,32,640]{2,1,0:T(8,128)(2,1)S(1)}, u32[]{:S(2)}, u32[]{:S(2)}) async-start(bf16[16,32,640]{2,1,0:T(8,128)(2,1)} %shard_map.124), calls=%async_computation.3 | async-start | bytes 1310720 | tf_op jit(solution)/shard_map/all_to_all | solution.py:265
  66.5 0.1 copy.18
  66.6 2.3 %broadcast_multiply_fusion = (bf16[20,16,20,16]{3,2,1,0:T(8,128)(2,1)}, bf16[20,16,20,16]{3,2,1,0:T(8,128)(2,1)}) fusion(bf16[20,20]{1,0:T(8,128)(2,1)S(1)} %copy-done.14, bf16[16,16]{1,0:T(8,128)(2,1)S(1)} %fusion, bf16[20,20]{1,0:T(8,128)(2,1)S(1)} %copy.18), kind=kLoop, calls=%fused_computation | loop fusion | flops 204800 | bytes 411712 | tf_op jit(solution)/shard_map/jit(kron)/mul | solution.py:280
  68.8 2.8 %mul.48.point_ref = bf16[320,320]{1,0:T(8,128)(2,1)S(1)} reshape(bf16[20,16,20,16]{3,2,1,0:T(8,128)(2,1)} %get-tuple-element.24) | data formatting | bytes 409600 | tf_op jit(solution)/shard_map/jit(kron)/mul | solution.py:281
  71.7 14.7 %all-to-all-done.3 = bf16[16,32,640]{2,1,0:T(8,128)(2,1)S(1)} async-done(((bf16[16,32,640]{2,1,0:T(8,128)(2,1)}), bf16[16,32,640]{2,1,0:T(8,128)(2,1)S(1)}, u32[]{:S(2)}, u32[]{:S(2)}) %all-to-all-start.3) | async-done | bytes 655392 | tf_op jit(solution)/shard_map/all_to_all | solution.py:265
  86.4 17.1 %shard_map.125 = (bf16[20,16,16,256]{3,2,1,0:T(8,128)(2,1)}, bf16[20,16,16,256]{3,2,1,0:T(8,128)(2,1)S(1)}, bf16[8,2,32,640]{3,2,1,0:T(8,128)(2,1)S(1)}) custom-call(bf16[8,2,32,640]{3,2,1,0:T(8,128)(2,1)S(1)} %bitcast.14, bf16[20,16,16,256]{3,2,1,0:T(8,128)(2,1)} %volume_ref.3, bf16[20,16,16,256]{3,2,1,0:T(8,128)(2,1)} %cotangent_ref.1, ...), custom_call_target="tpu_custom_call" | custom-call | flops 1500000000 | bytes 12000000 | tf_op jit(solution)/shard_map/pallas_call | solution.py:304
  103.6 1.5 copy-done.2
  105.0 25.6 %all_to_all.42.received_ref = bf16[16,32,640]{2,1,0:T(8,128)(2,1)S(1)} all-to-all(bf16[16,32,640]{2,1,0:T(8,128)(2,1)S(1)} %bitcast.16), channel_id=1, replica_groups=mesh['gx'=16,'gy'=16] {'gx'}, dimensions={0} | all-to-all | bytes 1310720 | tf_op jit(solution)/shard_map/all_to_all | solution.py:265
  130.6 0.4 shard_map.126
  131.0 10.5 %all_to_all.43.received_ref = bf16[16,8,320]{2,1,0:T(8,128)(2,1)S(1)} all-to-all(bf16[16,8,320]{2,1,0:T(8,128)(2,1)S(1)} %shard_map.126), channel_id=1, replica_groups=mesh['gx'=16,'gy'=16] {'gy'}, dimensions={0} | all-to-all | bytes 163840 | tf_op jit(solution)/shard_map/all_to_all | solution.py:270
  141.6 1.3 shard_map.127
  142.9 9.0 %all_to_all.44.received_ref = bf16[16,8,320]{2,1,0:T(8,128)(2,1)S(1)} all-to-all(bf16[16,8,320]{2,1,0:T(8,128)(2,1)S(1)} %get-tuple-element.13), channel_id=1, replica_groups=mesh['gx'=16,'gy'=16] {'gy'}, dimensions={0} | all-to-all | bytes 163840 | tf_op jit(solution)/shard_map/all_to_all | solution.py:270
  151.9 1.2 shard_map.128
  153.1 3.9 %all-to-all-start.7 = ((bf16[16,32,640]{2,1,0:T(8,128)(2,1)}), bf16[16,32,640]{2,1,0:T(8,128)(2,1)S(1)}, u32[]{:S(2)}, u32[]{:S(2)}) async-start(bf16[16,32,640]{2,1,0:T(8,128)(2,1)} %shard_map.128), calls=%async_computation.7 | async-start | bytes 1310720 | tf_op jit(solution)/shard_map/all_to_all | solution.py:265
  157.1 1.2 mul.51.point_ref
  158.3 0.1 shard_map.130
  158.4 1.8 reshape.54
  160.2 3.6 %copy.20 = f32[2,3,24,20,20]{2,0,4,3,1:T(2,128)} copy(f32[2,3,24,20,20]{2,1,4,3,0:T(4,128)} %reshape.54) | data formatting | bytes 460800
  163.7 13.1 %all-to-all-done.7 = bf16[16,32,640]{2,1,0:T(8,128)(2,1)S(1)} async-done(((bf16[16,32,640]{2,1,0:T(8,128)(2,1)}), bf16[16,32,640]{2,1,0:T(8,128)(2,1)S(1)}, u32[]{:S(2)}, u32[]{:S(2)}) %all-to-all-start.7) | async-done | bytes 655392 | tf_op jit(solution)/shard_map/all_to_all | solution.py:265
  176.8 3.8 %shard_map.129 = bf16[20,16,16,256]{3,2,1,0:T(8,128)(2,1)} custom-call(bf16[8,2,32,640]{3,2,1,0:T(8,128)(2,1)S(1)} %bitcast.13, bf16[20,16,16,256]{3,2,1,0:T(8,128)(2,1)S(1)} %copy-done.3, bf16[64,256]{1,0:T(8,128)(2,1)S(1)} %copy-done.8, bf16[320,320]{1,0:T(8,128)(2,1)S(1)} %mul.51.point_ref), custom_call_target="tpu_custom_call" | custom-call | flops 1300000000 | bytes 6000000 | tf_op jit(solution)/shard_map/pallas_call | solution.py:320
  (30 shorter events, 0.1 us)
Async XLA Ops:
  0.6 1.7 copy-start
  2.4 0.8 copy-start.7
  3.1 33.9 %copy-start.5 = (bf16[256,512]{1,0:T(8,128)(2,1)S(1)}, bf16[256,512]{1,0:T(8,128)(2,1)}, u32[]{:S(2)}) copy-start(bf16[256,512]{1,0:T(8,128)(2,1)} %constant.54.clone.matrix_ref) | copy-start | bytes 786436
  4.4 40.4 %copy-start.13 = (f32[2,3,24,20,20]{2,0,4,3,1:T(2,128)S(1)}, f32[2,3,24,20,20]{2,0,4,3,1:T(2,128)}, u32[]{:S(2)}) copy-start(f32[2,3,24,20,20]{2,0,4,3,1:T(2,128)} %param.11) | copy-start | bytes 691204
  38.1 12.6 %all-to-all-start.1 = ((bf16[16,8,320]{2,1,0:T(8,128)(2,1)}), bf16[16,8,320]{2,1,0:T(8,128)(2,1)S(1)}, u32[]{:S(2)}, u32[]{:S(2)}) async-start(bf16[16,8,320]{2,1,0:T(8,128)(2,1)} %shard_map.122), calls=%async_computation.1 | async-start | bytes 196608 | tf_op jit(solution)/shard_map/all_to_all | solution.py:270
  46.9 3.8 %copy-start.1 = (bf16[2048,256]{1,0:T(8,128)(2,1)S(1)}, bf16[2048,256]{1,0:T(8,128)(2,1)}, u32[]{:S(2)}) copy-start(bf16[2048,256]{1,0:T(8,128)(2,1)} %constant.56.clone.column_ref) | copy-start | bytes 3145732
  46.9 3.8 %copy-start.4 = (bf16[512,320]{1,0:T(8,128)(2,1)S(1)}, bf16[512,320]{1,0:T(8,128)(2,1)}, u32[]{:S(2)}) copy-start(bf16[512,320]{1,0:T(8,128)(2,1)} %constant.57.clone.order_ref) | copy-start | bytes 983044
  48.9 12.8 %copy-start.6 = (bf16[512,256]{1,0:T(8,128)(2,1)S(1)}, bf16[512,256]{1,0:T(8,128)(2,1)}, u32[]{:S(2)}) copy-start(bf16[512,256]{1,0:T(8,128)(2,1)} %constant.55.clone.matrix_ref) | copy-start | bytes 786436
  50.7 15.8 %copy-start.14 = (bf16[20,20]{1,0:T(8,128)(2,1)S(1)}, bf16[20,20]{1,0:T(8,128)(2,1)}, u32[]{:S(2)}) copy-start(bf16[20,20]{1,0:T(8,128)(2,1)} %param.12) | copy-start | bytes 2404
  52.0 10.9 %copy-start.9 = (f32[32,256]{1,0:T(8,128)}, f32[32,256]{1,0:T(8,128)S(1)}, u32[]{:S(2)}) copy-start(f32[32,256]{1,0:T(8,128)S(1)} %get-tuple-element.15.spectrum_ref) | copy-start | bytes 98308
  62.9 23.5 %all-to-all-start.3 = ((bf16[16,32,640]{2,1,0:T(8,128)(2,1)}), bf16[16,32,640]{2,1,0:T(8,128)(2,1)S(1)}, u32[]{:S(2)}, u32[]{:S(2)}) async-start(bf16[16,32,640]{2,1,0:T(8,128)(2,1)} %shard_map.124), calls=%async_computation.3 | async-start | bytes 1310720 | tf_op jit(solution)/shard_map/all_to_all | solution.py:265
  68.8 17.6 %copy-start.8 = (bf16[64,256]{1,0:T(8,128)(2,1)S(1)}, bf16[64,256]{1,0:T(8,128)(2,1)}, u32[]{:S(2)}) copy-start(bf16[64,256]{1,0:T(8,128)(2,1)} %constant.53.clone.depth_ref) | copy-start | bytes 98308
  68.8 17.6 %copy-start.11 = (f32[20]{0:T(128)S(1)}, f32[20]{0:T(128)}, u32[]{:S(2)}) copy-start(f32[20]{0:T(128)} %bias_ref.1) | copy-start | bytes 244
  103.5 1.5 copy-start.2
  142.9 14.1 %copy-start.12 = (bf16[20,16,20,16]{3,2,1,0:T(8,128)(2,1)S(1)}, bf16[20,16,20,16]{3,2,1,0:T(8,128)(2,1)}, u32[]{:S(2)}) copy-start(bf16[20,16,20,16]{3,2,1,0:T(8,128)(2,1)} %get-tuple-element.23) | copy-start | bytes 614404
  153.1 5.1 %copy-start.10 = (f32[32,256]{1,0:T(8,128)S(1)}, f32[32,256]{1,0:T(8,128)}, u32[]{:S(2)}) copy-start(f32[32,256]{1,0:T(8,128)} %copy-done.9) | copy-start | bytes 98308
  153.1 23.7 %all-to-all-start.7 = ((bf16[16,32,640]{2,1,0:T(8,128)(2,1)}), bf16[16,32,640]{2,1,0:T(8,128)(2,1)S(1)}, u32[]{:S(2)}, u32[]{:S(2)}) async-start(bf16[16,32,640]{2,1,0:T(8,128)(2,1)} %shard_map.128), calls=%async_computation.7 | async-start | bytes 1310720 | tf_op jit(solution)/shard_map/all_to_all | solution.py:265
  160.2 16.6 %copy-start.3 = (bf16[20,16,16,256]{3,2,1,0:T(8,128)(2,1)S(1)}, bf16[20,16,16,256]{3,2,1,0:T(8,128)(2,1)}, u32[]{:S(2)}) copy-start(bf16[20,16,16,256]{3,2,1,0:T(8,128)(2,1)} %copy-done.2) | copy-start | bytes 7864324

commit v2 on v1

--- a/solution.py
+++ b/solution.py
@@ -19,7 +19,7 @@
 M = 32
 G = 16
 CY = C * G
-VMEM = 48 * 1024 * 1024
+MIB = 1024 * 1024
 BF = jnp.bfloat16
 F32 = jnp.float32
 
@@ -102,8 +102,7 @@
     send_ref[:, 1] = jnp.concatenate(odds, 1).astype(BF)
 
 
-def synthesis(received_ref, g, e, depth):
-    rows = received_ref[...].astype(F32)
+def synthesis(rows, g, e, depth):
     even = rows[:, 0, 8 * g : 8 * g + 8]
     odd = rows[:, 1, 8 * g : 8 * g + 8]
     low = lax.broadcasted_iota(jnp.int32, even.shape, 1) < 4
@@ -187,46 +186,39 @@
 
 
 def activation(pre):
-    half = jnp.abs(pre) * (1.0 / math.sqrt(2.0))
-    bell = jnp.exp(-0.5 * pre * pre)
-    t = 1.0 / (1.0 + 0.3275911 * half)
-    poly = t * (0.254829592 + t * (-0.284496736 + t * (1.421413741 + t * (-1.453152027 + t * 1.061405429))))
-    tail = 0.5 * poly * bell
-    return jnp.where(pre < 0.0, tail, 1.0 - tail), bell * (1.0 / math.sqrt(2.0 * math.pi))
+    cumulative = 0.5 + 0.5 * lax.erf(pre * (1.0 / math.sqrt(2.0)))
+    density = jnp.exp(-0.5 * pre * pre) * (1.0 / math.sqrt(2.0 * math.pi))
+    return cumulative, density
 
 
 def forward_kernel(
-    received_ref, volume_ref, cotangent_ref, depth_ref, point_ref, bias_ref, output_ref, slope_ref, send_ref, pre_ref
+    received_ref, volume_ref, cotangent_ref, depth_ref, point_ref, bias_ref, output_ref, slope_ref, send_ref
 ):
     depth = depth_ref[...]
     point = point_ref[...]
+    rows = received_ref[...].astype(F32)
     for g in range(2):
         for e in range(2):
-            pre_ref[...] = synthesis(received_ref, g, e, depth)
+            spectral = synthesis(rows, g, e, depth)
             for h in range(2):
                 x = 4 * g + 2 * h + e
-                pre_ref[h * CY : (h + 1) * CY] += dot(point, volume_ref[:, x].reshape(CY, L))
-
-                def step(n, carry):
-                    for k in range(2):
-                        c = n * 2 + k
-                        pre = pre_ref[pl.ds(pl.multiple_of(h * CY + c * G, G), G)] + bias_ref[c]
-                        cumulative, density = activation(pre)
-                        output_ref[c, x] = (pre * cumulative).astype(BF)
-                        slope = cotangent_ref[c, x].astype(F32) * (cumulative + pre * density)
-                        slope_ref[c, x] = slope.astype(BF)
-                    return carry
-
-                lax.fori_loop(0, C // 2, step, 0)
+                total = spectral[h * CY : (h + 1) * CY] + dot(point, volume_ref[:, x].reshape(CY, L))
+                for c in range(C):
+                    pre = total[c * G : (c + 1) * G] + bias_ref[c]
+                    cumulative, density = activation(pre)
+                    output_ref[c, x] = (pre * cumulative).astype(BF)
+                    slope = cotangent_ref[c, x].astype(F32) * (cumulative + pre * density)
+                    slope_ref[c, x] = slope.astype(BF)
     send_planes(lambda x: slope_ref[:, x].reshape(CY, L), depth, send_ref)
 
 
 def backward_kernel(received_ref, slope_ref, depth_ref, point_ref, output_ref):
     depth = depth_ref[...]
     point = point_ref[...]
+    rows = received_ref[...].astype(F32)
     for g in range(2):
         for e in range(2):
-            spectral = synthesis(received_ref, g, e, depth)
+            spectral = synthesis(rows, g, e, depth)
             for h in range(2):
                 x = 4 * g + 2 * h + e
                 total = spectral[h * CY : (h + 1) * CY] + dot(point, slope_ref[:, x].reshape(CY, L))
@@ -246,7 +238,7 @@
 MODES = jax.ShapeDtypeStruct((32, 256), F32)
 
 
-def call(kernel, out_shape, in_specs=None, out_specs=None, grid=(), scratch=(), flops=0, moved=0):
+def call(kernel, out_shape, in_specs=None, out_specs=None, grid=(), scratch=(), flops=0, moved=0, room=16):
     extra = {}
     if in_specs is not None:
         extra = {"in_specs": in_specs, "out_specs": out_specs}
@@ -255,7 +247,7 @@
         out_shape=out_shape,
         grid=grid,
         scratch_shapes=scratch,
-        compiler_params=pltpu.CompilerParams(vmem_limit_bytes=VMEM),
+        compiler_params=pltpu.CompilerParams(vmem_limit_bytes=room * MIB),
         cost_estimate=pl.CostEstimate(flops=int(flops), bytes_accessed=moved, transcendentals=0),
         **extra,
     )
@@ -285,7 +277,7 @@
     weight = jnp.pad(weight, ((0, 0), (0, 0), (0, 0), (0, 128 - 3 * K)))
 
     depth_call = call(
-        depth_kernel, BIG, [PLANES, whole((64, L))], BIG_ROWS, (2,), flops=170e6, moved=3300000
+        depth_kernel, BIG, [PLANES, whole((64, L))], BIG_ROWS, (2,), flops=170e6, moved=3300000, room=60
     )
     row_call = call(row_kernel, SMALL, flops=170e6, moved=1000000)
     row_back_call = call(row_back_kernel, jax.ShapeDtypeStruct((G, 32, 2 * CY), BF), flops=170e6, moved=1000000)
@@ -297,6 +289,7 @@
     gradient_call = call(gradient_kernel, jax.ShapeDtypeStruct((2, C, C, 128), F32), flops=1e6, moved=1000000)
 
     received = exchange_rows(depth_call(saturation, depth))
+    received, weight = lax.optimization_barrier((received, weight))
     received = exchange_columns(row_call(received, rows))
     sent, spectrum = mix_call(received, order, columns, weight, factor)
     received = exchange_columns(sent)
@@ -307,9 +300,10 @@
         [BIG_ROWS, PLANES, PLANES, whole((64, L)), whole((CY, CY)), SMEM],
         (PLANES, PLANES, BIG_ROWS),
         (2,),
-        [pltpu.VMEM((2 * CY, L), F32)],
+        (),
         1500e6,
         12000000,
+        60,
     )(received.reshape(BIG.shape), saturation, cotangent, depth, point, pointwise_bias)
     received = exchange_rows(sent)
     received = exchange_columns(row_call(received, rows))
@@ -326,6 +320,7 @@
         (),
         1300e6,
         6000000,
+        20,
     )(received.reshape(BIG.shape), slope, depth, point_back)
     gradient = jnp.transpose(gradient[..., : 3 * K], (0, 3, 1, 2)).reshape(2, 3, K, C, C)
     return layer_output, input_gradient, gradient

time: 182 us -> 171 us (0.940)
  blocking collectives: 87.3 us -> 54.1 us
  waiting for transfers between devices: 29.5 us -> 45.3 us
  starting transfers between devices: 14.2 us -> 26.4 us
  Pallas kernels: 28.8 us -> 21.9 us
    all_to_all x2 -> x1, blocking collectives: 58.1 us -> 24.3 us  [exchange_rows(): lax.all_to_all(packed.reshape(G, 32, 2 * CY), 'gx', 0, 0, tiled=True)]
    all_to_all x2 -> x3, waiting for transfers between devices: 27.8 us -> 39.4 us  [exchange_rows(): lax.all_to_all(packed.reshape(G, 32, 2 * CY), 'gx', 0, 0, tiled=True)]
    all_to_all x2 -> x3, starting transfers between devices: 7.5 us -> 18.9 us  [exchange_rows(): lax.all_to_all(packed.reshape(G, 32, 2 * CY), 'gx', 0, 0, tiled=True)]
    pallas_call x1, Pallas kernels: 17.1 us -> 8.35 us  [shards(): call(forward_kernel, (FIELD, FIELD, BIG), [BIG_ROWS, PLANES, PLANES, whol...]
    all_to_all x1, waiting for transfers between devices: 1.76 us -> 5.85 us  [exchange_columns(): return lax.all_to_all(packed, 'gy', 0, 0, tiled=True)]
    unnamed x31 -> x19, local copies, waits for them, and re-layouts: 7.59 us -> 4.43 us
    pallas_call x1, Pallas kernels: 1.29 us -> 3.21 us  [shards(): received = exchange_rows(depth_call(saturation, depth))]
  transfers between devices with their start and end apart: 3 -> 4, of which waited for: 3 -> 4; matrix products, arithmetic and copies ran while one was open for 9% -> 12% of each run, Pallas kernels for 0% -> 0%
where the time goes in v2:
time: 171 us; the launch traced here: 169 us
  blocking collectives  54.1 us (32%)
  waiting for transfers between devices  45.3 us (26%)
  starting transfers between devices  26.4 us (15%)
  Pallas kernels  21.9 us (13%)
  local copies, waits for them, and re-layouts  18.4 us (11%)
  other arithmetic  2.27 us (1%)
    all_to_all x3, waiting for transfers between devices, exchange_rows(): lax.all_to_all(packed.reshape(G, 32, 2 * CY), 'gx', 0, 0, tiled=True)  39.4 us
    all_to_all x3, blocking collectives, exchange_columns(): return lax.all_to_all(packed, 'gy', 0, 0, tiled=True)  29.7 us
    all_to_all x1, blocking collectives, exchange_rows(): lax.all_to_all(packed.reshape(G, 32, 2 * CY), 'gx', 0, 0, tiled=True)  24.3 us
    all_to_all x3, starting transfers between devices, exchange_rows(): lax.all_to_all(packed.reshape(G, 32, 2 * CY), 'gx', 0, 0, tiled=True)  18.9 us
    pallas_call x1, Pallas kernels, shards(): call(forward_kernel, (FIELD, FIELD, BIG), [BIG_ROWS, PLANES, PLANES, whol...  8.35 us
    all_to_all x1, starting transfers between devices, exchange_columns(): return lax.all_to_all(packed, 'gy', 0, 0, tiled=True)  7.48 us
    all_to_all x1, waiting for transfers between devices, exchange_columns(): return lax.all_to_all(packed, 'gy', 0, 0, tiled=True)  5.85 us
    reshape x2, local copies, waits for them, and re-layouts, shards(): spectral_weight.reshape(2, 3 * K, C, C)  4.7 us
  transfers between devices with their start and end apart: 4, of which 4 were waited for; matrix products, arithmetic and copies ran while one was open for 12% of the time, Pallas kernels for 0%

profile of v2, /device:TPU:1, one launch (start us, length us, event | category | flops | bytes accessed | tf_op | source)
XLA Modules:
  0.0 169.1 jit_solution(14746352099488315726)
XLA Ops:
  0.6 3.2 %shard_map.121 = bf16[8,2,32,640]{3,2,1,0:T(8,128)(2,1)} custom-call(bf16[20,16,16,256]{3,2,1,0:T(8,128)(2,1)} %volume_ref.3, bf16[64,256]{1,0:T(8,128)(2,1)} %constant.53.clone.depth_ref), custom_call_target="tpu_custom_call" | custom-call | flops 170000000 | bytes 3300000 | tf_op jit(solution)/shard_map/pallas_call | solution.py:291
  3.9 11.6 %all-to-all-start = ((bf16[16,32,640]{2,1,0:T(8,128)(2,1)}), bf16[16,32,640]{2,1,0:T(8,128)(2,1)S(1)}, u32[]{:S(2)}, u32[]{:S(2)}) async-start(bf16[16,32,640]{2,1,0:T(8,128)(2,1)} %bitcast.15), calls=%async_computation | async-start | bytes 1310720 | tf_op jit(solution)/shard_map/all_to_all | solution.py:257
  15.4 2.0 %copy.21 = f32[2,3,24,20,20]{2,1,4,3,0:T(4,128)} copy(f32[2,3,24,20,20]{2,0,4,3,1:T(2,128)S(1)} %copy-done.7) | data formatting | bytes 460800 | tf_op jit(solution)/shard_map/reshape | solution.py:276
  17.5 2.7 %reshape.53 = f32[2,72,20,20]{1,3,2,0:T(8,128)} reshape(f32[2,3,24,20,20]{2,1,4,3,0:T(4,128)} %copy.21) | data formatting | bytes 460800 | tf_op jit(solution)/shard_map/reshape | solution.py:276
  20.2 1.1 pad.4.weight_ref
  21.2 13.9 %all-to-all-done.received_ref = bf16[16,32,640]{2,1,0:T(8,128)(2,1)S(1)} async-done(((bf16[16,32,640]{2,1,0:T(8,128)(2,1)}), bf16[16,32,640]{2,1,0:T(8,128)(2,1)S(1)}, u32[]{:S(2)}, u32[]{:S(2)}) %all-to-all-start) | async-done | bytes 655392 | tf_op jit(solution)/shard_map/all_to_all | solution.py:257
  35.1 1.1 shard_map.122
  36.2 7.5 %all-to-all-start.1 = ((bf16[16,8,320]{2,1,0:T(8,128)(2,1)}), bf16[16,8,320]{2,1,0:T(8,128)(2,1)S(1)}, u32[]{:S(2)}, u32[]{:S(2)}) async-start(bf16[16,8,320]{2,1,0:T(8,128)(2,1)} %shard_map.122), calls=%async_computation.1 | async-start | bytes 196608 | tf_op jit(solution)/shard_map/all_to_all | solution.py:262
  43.7 5.8 %all-to-all-done.1.received_ref = bf16[16,8,320]{2,1,0:T(8,128)(2,1)S(1)} async-done(((bf16[16,8,320]{2,1,0:T(8,128)(2,1)}), bf16[16,8,320]{2,1,0:T(8,128)(2,1)S(1)}, u32[]{:S(2)}, u32[]{:S(2)}) %all-to-all-start.1) | async-done | bytes 81952 | tf_op jit(solution)/shard_map/all_to_all | solution.py:262
  49.6 1.3 shard_map.123
  50.9 8.9 %all_to_all.40.received_ref = bf16[16,8,320]{2,1,0:T(8,128)(2,1)S(1)} all-to-all(bf16[16,8,320]{2,1,0:T(8,128)(2,1)S(1)} %get-tuple-element.14), channel_id=1, replica_groups=mesh['gx'=16,'gy'=16] {'gy'}, dimensions={0} | all-to-all | bytes 163840 | tf_op jit(solution)/shard_map/all_to_all | solution.py:262
  59.7 1.2 shard_map.124
  60.9 3.6 %all-to-all-start.3 = ((bf16[16,32,640]{2,1,0:T(8,128)(2,1)}), bf16[16,32,640]{2,1,0:T(8,128)(2,1)S(1)}, u32[]{:S(2)}, u32[]{:S(2)}) async-start(bf16[16,32,640]{2,1,0:T(8,128)(2,1)} %shard_map.124), calls=%async_computation.3 | async-start | bytes 1310720 | tf_op jit(solution)/shard_map/all_to_all | solution.py:257
  64.5 0.1 copy.18
  64.6 2.3 %broadcast_multiply_fusion = (bf16[20,16,20,16]{3,2,1,0:T(8,128)(2,1)}, bf16[20,16,20,16]{3,2,1,0:T(8,128)(2,1)}) fusion(bf16[20,20]{1,0:T(8,128)(2,1)S(1)} %copy-done.8, bf16[16,16]{1,0:T(8,128)(2,1)S(1)} %fusion, bf16[20,20]{1,0:T(8,128)(2,1)S(1)} %copy.18), kind=kLoop, calls=%fused_computation | loop fusion | flops 204800 | bytes 411712 | tf_op jit(solution)/shard_map/jit(kron)/mul | solution.py:272
  66.9 3.5 %mul.48.point_ref = bf16[320,320]{1,0:T(8,128)(2,1)} reshape(bf16[20,16,20,16]{3,2,1,0:T(8,128)(2,1)} %get-tuple-element.28) | data formatting | bytes 409600 | tf_op jit(solution)/shard_map/jit(kron)/mul | solution.py:273
  70.4 14.1 %all-to-all-done.3 = bf16[16,32,640]{2,1,0:T(8,128)(2,1)S(1)} async-done(((bf16[16,32,640]{2,1,0:T(8,128)(2,1)}), bf16[16,32,640]{2,1,0:T(8,128)(2,1)S(1)}, u32[]{:S(2)}, u32[]{:S(2)}) %all-to-all-start.3) | async-done | bytes 655392 | tf_op jit(solution)/shard_map/all_to_all | solution.py:257
  84.5 0.8 copy-done.6
  85.3 8.4 %shard_map.125 = (bf16[20,16,16,256]{3,2,1,0:T(8,128)(2,1)}, bf16[20,16,16,256]{3,2,1,0:T(8,128)(2,1)}, bf16[8,2,32,640]{3,2,1,0:T(8,128)(2,1)}) custom-call(bf16[8,2,32,640]{3,2,1,0:T(8,128)(2,1)} %bitcast.14, bf16[20,16,16,256]{3,2,1,0:T(8,128)(2,1)} %volume_ref.3, bf16[20,16,16,256]{3,2,1,0:T(8,128)(2,1)} %cotangent_ref.1, ...), custom_call_target="tpu_custom_call" | custom-call | flops 1500000000 | bytes 12000000 | tf_op jit(solution)/shard_map/pallas_call | solution.py:297
  93.6 24.3 %all_to_all.41.received_ref = bf16[16,32,640]{2,1,0:T(8,128)(2,1)S(1)} all-to-all(bf16[16,32,640]{2,1,0:T(8,128)(2,1)} %bitcast.17), channel_id=1, replica_groups=mesh['gx'=16,'gy'=16] {'gx'}, dimensions={0} | all-to-all | bytes 1310720 | tf_op jit(solution)/shard_map/all_to_all | solution.py:257
  118.0 0.4 shard_map.126
  118.4 12.0 %all_to_all.42.received_ref = bf16[16,8,320]{2,1,0:T(8,128)(2,1)S(1)} all-to-all(bf16[16,8,320]{2,1,0:T(8,128)(2,1)S(1)} %shard_map.126), channel_id=1, replica_groups=mesh['gx'=16,'gy'=16] {'gy'}, dimensions={0} | all-to-all | bytes 163840 | tf_op jit(solution)/shard_map/all_to_all | solution.py:262
  130.4 1.3 shard_map.127
  131.7 8.9 %all_to_all.43.received_ref = bf16[16,8,320]{2,1,0:T(8,128)(2,1)S(1)} all-to-all(bf16[16,8,320]{2,1,0:T(8,128)(2,1)S(1)} %get-tuple-element.17), channel_id=1, replica_groups=mesh['gx'=16,'gy'=16] {'gy'}, dimensions={0} | all-to-all | bytes 163840 | tf_op jit(solution)/shard_map/all_to_all | solution.py:262
  140.6 1.2 shard_map.128
  141.8 3.8 %all-to-all-start.7 = ((bf16[16,32,640]{2,1,0:T(8,128)(2,1)}), bf16[16,32,640]{2,1,0:T(8,128)(2,1)S(1)}, u32[]{:S(2)}, u32[]{:S(2)}) async-start(bf16[16,32,640]{2,1,0:T(8,128)(2,1)} %shard_map.128), calls=%async_computation.7 | async-start | bytes 1310720 | tf_op jit(solution)/shard_map/all_to_all | solution.py:257
  145.6 2.8 %mul.51.point_ref = bf16[320,320]{1,0:T(8,128)(2,1)S(1)} reshape(bf16[20,16,20,16]{3,2,1,0:T(8,128)(2,1)} %get-tuple-element.27) | data formatting | bytes 409600 | tf_op jit(solution)/shard_map/jit(kron)/mul | solution.py:272
  148.5 0.1 shard_map.130
  148.6 1.8 %reshape.54 = f32[2,3,24,20,20]{2,1,4,3,0:T(4,128)} reshape(f32[2,72,20,20]{1,3,2,0:T(8,128)S(1)} %slice_bitcast_fusion) | data formatting | bytes 460800 | tf_op jit(solution)/shard_map/reshape | solution.py:325
  150.3 3.6 %copy.20 = f32[2,3,24,20,20]{2,0,4,3,1:T(2,128)} copy(f32[2,3,24,20,20]{2,1,4,3,0:T(4,128)} %reshape.54) | data formatting | bytes 460800
  153.9 11.5 %all-to-all-done.7 = bf16[16,32,640]{2,1,0:T(8,128)(2,1)S(1)} async-done(((bf16[16,32,640]{2,1,0:T(8,128)(2,1)}), bf16[16,32,640]{2,1,0:T(8,128)(2,1)S(1)}, u32[]{:S(2)}, u32[]{:S(2)}) %all-to-all-start.7) | async-done | bytes 655392 | tf_op jit(solution)/shard_map/all_to_all | solution.py:257
  165.4 3.8 %shard_map.129 = bf16[20,16,16,256]{3,2,1,0:T(8,128)(2,1)} custom-call(bf16[8,2,32,640]{3,2,1,0:T(8,128)(2,1)S(1)} %bitcast.13, bf16[20,16,16,256]{3,2,1,0:T(8,128)(2,1)S(1)} %copy-done.1, bf16[64,256]{1,0:T(8,128)(2,1)S(1)} %copy-done.5, bf16[320,320]{1,0:T(8,128)(2,1)S(1)} %mul.51.point_ref), custom_call_target="tpu_custom_call" | custom-call | flops 1300000000 | bytes 6000000 | tf_op jit(solution)/shard_map/pallas_call | solution.py:314
  (19 shorter events, 0.1 us)
Async XLA Ops:
  0.6 14.8 %copy-start.7 = (f32[2,3,24,20,20]{2,0,4,3,1:T(2,128)S(1)}, f32[2,3,24,20,20]{2,0,4,3,1:T(2,128)}, u32[]{:S(2)}) copy-start(f32[2,3,24,20,20]{2,0,4,3,1:T(2,128)} %param.11) | copy-start | bytes 691204
  3.9 31.3 %all-to-all-start = ((bf16[16,32,640]{2,1,0:T(8,128)(2,1)}), bf16[16,32,640]{2,1,0:T(8,128)(2,1)S(1)}, u32[]{:S(2)}, u32[]{:S(2)}) async-start(bf16[16,32,640]{2,1,0:T(8,128)(2,1)} %bitcast.15), calls=%async_computation | async-start | bytes 1310720 | tf_op jit(solution)/shard_map/all_to_all | solution.py:257
  17.5 17.7 %copy-start.4 = (bf16[256,512]{1,0:T(8,128)(2,1)S(1)}, bf16[256,512]{1,0:T(8,128)(2,1)}, u32[]{:S(2)}) copy-start(bf16[256,512]{1,0:T(8,128)(2,1)} %constant.54.clone.matrix_ref) | copy-start | bytes 786436
  17.5 32.1 %copy-start = (bf16[2048,256]{1,0:T(8,128)(2,1)S(1)}, bf16[2048,256]{1,0:T(8,128)(2,1)}, u32[]{:S(2)}) copy-start(bf16[2048,256]{1,0:T(8,128)(2,1)} %constant.56.clone.column_ref) | copy-start | bytes 3145732
  17.5 32.1 %copy-start.2 = (bf16[512,320]{1,0:T(8,128)(2,1)S(1)}, bf16[512,320]{1,0:T(8,128)(2,1)}, u32[]{:S(2)}) copy-start(bf16[512,320]{1,0:T(8,128)(2,1)} %constant.57.clone.order_ref) | copy-start | bytes 983044
  21.2 38.5 %copy-start.3 = (bf16[512,256]{1,0:T(8,128)(2,1)S(1)}, bf16[512,256]{1,0:T(8,128)(2,1)}, u32[]{:S(2)}) copy-start(bf16[512,256]{1,0:T(8,128)(2,1)} %constant.55.clone.matrix_ref) | copy-start | bytes 786436
  36.2 13.3 %all-to-all-start.1 = ((bf16[16,8,320]{2,1,0:T(8,128)(2,1)}), bf16[16,8,320]{2,1,0:T(8,128)(2,1)S(1)}, u32[]{:S(2)}, u32[]{:S(2)}) async-start(bf16[16,8,320]{2,1,0:T(8,128)(2,1)} %shard_map.122), calls=%async_computation.1 | async-start | bytes 196608 | tf_op jit(solution)/shard_map/all_to_all | solution.py:262
  49.6 15.0 %copy-start.8 = (bf16[20,20]{1,0:T(8,128)(2,1)S(1)}, bf16[20,20]{1,0:T(8,128)(2,1)}, u32[]{:S(2)}) copy-start(bf16[20,20]{1,0:T(8,128)(2,1)} %param.12) | copy-start | bytes 2404
  60.9 23.5 %all-to-all-start.3 = ((bf16[16,32,640]{2,1,0:T(8,128)(2,1)}), bf16[16,32,640]{2,1,0:T(8,128)(2,1)S(1)}, u32[]{:S(2)}, u32[]{:S(2)}) async-start(bf16[16,32,640]{2,1,0:T(8,128)(2,1)} %shard_map.124), calls=%async_computation.3 | async-start | bytes 1310720 | tf_op jit(solution)/shard_map/all_to_all | solution.py:257
  84.5 0.8 copy-start.6
  141.8 23.5 %all-to-all-start.7 = ((bf16[16,32,640]{2,1,0:T(8,128)(2,1)}), bf16[16,32,640]{2,1,0:T(8,128)(2,1)S(1)}, u32[]{:S(2)}, u32[]{:S(2)}) async-start(bf16[16,32,640]{2,1,0:T(8,128)(2,1)} %shard_map.128), calls=%async_computation.7 | async-start | bytes 1310720 | tf_op jit(solution)/shard_map/all_to_all | solution.py:257
  150.3 15.0 %copy-start.1 = (bf16[20,16,16,256]{3,2,1,0:T(8,128)(2,1)S(1)}, bf16[20,16,16,256]{3,2,1,0:T(8,128)(2,1)}, u32[]{:S(2)}) copy-start(bf16[20,16,16,256]{3,2,1,0:T(8,128)(2,1)} %get-tuple-element.18.slope_ref) | copy-start | bytes 7864324
  150.3 15.0 %copy-start.5 = (bf16[64,256]{1,0:T(8,128)(2,1)S(1)}, bf16[64,256]{1,0:T(8,128)(2,1)}, u32[]{:S(2)}) copy-start(bf16[64,256]{1,0:T(8,128)(2,1)} %constant.53.clone.depth_ref) | copy-start | bytes 98308

commit v3 on v2

v3 whole, which is shorter than its diff:
```python
import functools
import math

import jax
import jax.numpy as jnp
import numpy as np
from jax import lax
from jax.experimental import pallas as pl
from jax.experimental.pallas import tpu as pltpu
from jax.sharding import PartitionSpec as P

C = 20
Z = 32
T_SIZE = 8
L = 256
K = 24
KZ = 8
KT = 4
M = 32
G = 16
CY = C * G
MIB = 1024 * 1024
BF = jnp.bfloat16
F32 = jnp.float32


def kept_frequency(kept_count):
    position = np.arange(kept_count)
    return np.where(position < kept_count // 2, position, position - kept_count)


def axis_table():
    product = (np.arange(L)[:, None] * kept_frequency(K)[None, :]) % L
    angle = product.astype(np.float32) * np.float32(2.0 * math.pi / L)
    cosine = np.cos(angle) * np.float32(1.0 / math.sqrt(L))
    sine = np.sin(angle) * np.float32(1.0 / math.sqrt(L))
    return np.stack([np.stack([cosine, -sine], -1), np.stack([sine, cosine], -1)], 1)


def depth_table():
    cell = np.arange(Z * T_SIZE)
    depth = ((cell // T_SIZE)[:, None] * kept_frequency(KZ)[None, :] % Z).astype(np.float32) / np.float32(Z)
    time = ((cell % T_SIZE)[:, None] * np.arange(KT)[None, :] % T_SIZE).astype(np.float32) / np.float32(T_SIZE)
    angle = (depth[:, :, None] + time[:, None, :]).reshape(Z * T_SIZE, M) * np.float32(2.0 * math.pi)
    scale = np.float32(1.0 / math.sqrt(Z * T_SIZE))
    table = np.stack([np.cos(angle) * scale, -np.sin(angle) * scale], -1)
    return table.reshape(Z * T_SIZE, 2 * M).T


def row_matrix():
    table = axis_table().reshape(G, 4, 2, 2, 2, 8, 3, 2)
    out = np.zeros((2, 2, 8, 8, G, 4, 2, 2, 2), np.float32)
    part = table.transpose(2, 5, 6, 7, 0, 1, 3, 4).reshape(2, 8, 6, G, 4, 2, 2)
    for pair in range(2):
        out[:, pair, :, :6, :, :, :, pair, :] = part
    return out.reshape(256, 512)


def column_matrix():
    table = axis_table().reshape(G, G, 2, K, 2)
    out = np.zeros((G, G, 8, 2, 128), np.float32)
    for t in range(3):
        for r in range(2):
            out[:, :, 2 * t + r, :, t * K : (t + 1) * K] = table[:, :, r].transpose(1, 0, 3, 2)
    return out.reshape(2048, 256)


def order_matrix():
    out = np.zeros((G, 32, C, G), np.float32)
    for y in range(G):
        for c in range(C):
            out[y, c, c, y] = 1.0
    return out.reshape(512, CY)


def dot(a, b, contract=(1, 0)):
    return lax.dot_general(
        a, b, (((contract[0],), (contract[1],)), ((), ())), preferred_element_type=F32
    )


def pack(first, second):
    first = first.reshape(8, 8, 2 * CY)
    second = second.reshape(8, 8, 2 * CY)
    low = lax.broadcasted_iota(jnp.int32, first.shape, 1) < 4
    even = jnp.where(low, first, pltpu.roll(second, 4, 1))
    odd = jnp.where(low, pltpu.roll(first, 4, 1), second)
    return even, odd


def packed_planes(plane, depth):
    return pack(*[dot(depth, jnp.concatenate([plane(e), plane(2 + e)], 0), (1, 1)) for e in range(2)])


def send_planes(tiles, send_ref, rows):
    for parity in range(2):
        send_ref[:, parity, rows] = jnp.concatenate([tiles[0][parity], tiles[1][parity]], 1).astype(BF)


def synthesis(rows, g, e, depth):
    even = rows[:, 0, 8 * g : 8 * g + 8]
    odd = rows[:, 1, 8 * g : 8 * g + 8]
    low = lax.broadcasted_iota(jnp.int32, even.shape, 1) < 4
    if e == 0:
        both = jnp.where(low, even, pltpu.roll(odd, 4, 1))
    else:
        both = jnp.where(low, pltpu.roll(even, 4, 1), odd)
    return dot(both.reshape(64, 2 * CY).astype(BF), depth, (0, 0))


def depth_kernel(volume_ref, depth_ref, send_ref):
    depth = depth_ref[...]
    tiles = [packed_planes(lambda k: volume_ref[:, 4 * g + k].reshape(CY, L), depth) for g in range(2)]
    send_planes(tiles, send_ref, slice(0, 16))


def row_kernel(received_ref, matrix_ref, send_ref):
    product = dot(matrix_ref[...], received_ref[...].reshape(512, 2 * CY))
    total = product[:128] + pltpu.roll(product[128:], CY, 1)
    send_ref[...] = total[:, :CY].reshape(G, 8, CY).astype(BF)


def row_back_kernel(received_ref, matrix_ref, send_ref):
    modes = received_ref[...].astype(F32).reshape(128, CY)
    zeros = jnp.zeros((128, CY), F32)
    upper = jnp.concatenate([modes, zeros], 1)
    lower = jnp.concatenate([zeros, modes], 1)
    both = jnp.concatenate([upper, lower], 0).astype(BF)
    send_ref[...] = dot(matrix_ref[...], both).reshape(G, 32, 2 * CY).astype(BF)


def column_analysis(received_ref, order_ref, column_ref):
    rows = dot(order_ref[...], received_ref[...].reshape(128, CY), (1, 1))
    lanes = jnp.concatenate([rows[32 * y : 32 * y + 32] for y in range(G)], 1)
    return dot(lanes.astype(BF), column_ref[...])


def column_synthesis(modes, order_ref, column_ref, send_ref):
    lanes = dot(modes.astype(BF), column_ref[...], (1, 1))
    rows = jnp.concatenate([lanes[:, 128 * y : 128 * y + 128] for y in range(G)], 0)
    send_ref[...] = dot(rows.astype(BF), order_ref[...], (0, 0)).reshape(G, 8, CY).astype(BF)


def weight_rows(weight_ref, i):
    spare = jnp.zeros((2 * C, 128 - 3 * K), F32)
    return jnp.concatenate([weight_ref[0, i], weight_ref[1, i], weight_ref[2, i], spare], 1)


def partner(rows):
    part = lax.broadcasted_iota(jnp.int32, rows.shape, 0) % 2
    return part == 0, jnp.where(part == 0, pltpu.roll(rows, 2 * C - 1, 0), pltpu.roll(rows, 1, 0))


def mode_factor():
    pair = lax.axis_index("gx") * 2 + lax.axis_index("gy") // 8
    return jnp.where(pair % KT == 0, 1.0, 2.0).astype(F32)


def mix_kernel(
    received_ref, order_ref, column_ref, weight_ref, send_ref, spectrum_ref, mixed_ref, parts_ref
):
    spectrum_ref[...] = column_analysis(received_ref, order_ref, column_ref)
    by_real = jnp.zeros((2 * C, 128), F32)
    by_imag = jnp.zeros((2 * C, 128), F32)
    for i in range(C):
        weight = weight_rows(weight_ref, i)
        by_real += weight * spectrum_ref[i : i + 1, :128]
        by_imag += weight * spectrum_ref[i : i + 1, 128:]
    is_real, other = partner(by_imag)
    parts_ref[...] = (by_real + jnp.where(is_real, -other, other)) * mode_factor()
    mixed_ref[...] = jnp.zeros((32, 256), F32)
    mixed_ref[:C, :128] = parts_ref[pl.ds(0, C, stride=2), :]
    mixed_ref[:C, 128:] = parts_ref[pl.ds(1, C, stride=2), :]
    column_synthesis(mixed_ref[...], order_ref, column_ref, send_ref)


def back_mix_kernel(
    received_ref, order_ref, column_ref, weight_ref, spectrum_ref,
    send_ref, gradient_ref, mixed_ref, parts_ref,
):
    mixed_ref[...] = column_analysis(received_ref, order_ref, column_ref) * mode_factor()
    parts_ref[pl.ds(0, C, stride=2), :] = mixed_ref[:C, :128]
    parts_ref[pl.ds(1, C, stride=2), :] = mixed_ref[:C, 128:]
    upstream = parts_ref[...]
    is_real, other = partner(upstream)
    turned = jnp.where(is_real, other, -other)
    mixed_ref[...] = jnp.zeros((32, 256), F32)
    for i in range(C):
        weight = weight_rows(weight_ref, i)
        mixed_ref[i : i + 1, :128] = jnp.sum(weight * upstream, 0, keepdims=True)
        mixed_ref[i : i + 1, 128:] = jnp.sum(weight * turned, 0, keepdims=True)
    column_synthesis(mixed_ref[...], order_ref, column_ref, send_ref)
    for i in range(C):
        gradient = upstream * spectrum_ref[i : i + 1, :128] + turned * spectrum_ref[i : i + 1, 128:]
        for t in range(3):
            gradient_ref[t, i] = gradient[:, t * K : (t + 1) * K]


def activation(pre):
    cumulative = 0.5 + 0.5 * lax.erf(pre * (1.0 / math.sqrt(2.0)))
    density = jnp.exp(-0.5 * pre * pre) * (1.0 / math.sqrt(2.0 * math.pi))
    return cumulative, density


def spread_point(point_ref, side):
    row = lax.broadcasted_iota(jnp.int32, (CY, C), 0) // G
    repeat = jnp.where(row == lax.broadcasted_iota(jnp.int32, (CY, C), 1), 1.0, 0.0).astype(BF)
    tall = dot(repeat, point_ref[...], (1, 1 - side)).astype(BF)
    wide = dot(tall, repeat, (1, 1))
    row = lax.broadcasted_iota(jnp.int32, (CY, CY), 0) % G
    column = lax.broadcasted_iota(jnp.int32, (CY, CY), 1) % G
    return jnp.where(row == column, wide, 0.0).astype(BF)


def leave(made_ref, output_ref, left, block):
    planes = pl.ds(4 * block, 4)
    return pltpu.make_async_copy(made_ref.at[:, planes], output_ref.at[:, planes], left.at[block])


def half_rows(received_ref, half):
    return received_ref[:, :, pl.ds(pl.multiple_of(16 * half, 16), 16), :].astype(F32)


def forward_kernel(
    received_ref, volume_ref, cotangent_ref, depth_ref, point_ref, bias_ref,
    output_ref, slope_ref, send_ref, wide_ref, made_ref, left,
):
    depth = depth_ref[...]
    wide_ref[...] = spread_point(point_ref, 0)

    def step(half, carry):
        rows = half_rows(received_ref, half)
        point = wide_ref[...]
        tiles = []
        for g in range(2):
            first = 8 * half + 4 * g
            for e in range(2):
                spectral = synthesis(rows, g, e, depth)
                for h in range(2):
                    x = first + 2 * h + e
                    total = spectral[h * CY : (h + 1) * CY] + dot(point, volume_ref[:, x].reshape(CY, L))
                    for c in range(C):
                        pre = total[c * G : (c + 1) * G] + bias_ref[c]
                        cumulative, density = activation(pre)
                        made_ref[c, x] = (pre * cumulative).astype(BF)
                        slope = cotangent_ref[c, x].astype(F32) * (cumulative + pre * density)
                        slope_ref[c, x] = slope.astype(BF)
            leave(made_ref, output_ref, left, 2 * half + g).start()
            tiles.append(packed_planes(lambda k: slope_ref[:, first + k].reshape(CY, L), depth))
        send_planes(tiles, send_ref, pl.ds(pl.multiple_of(16 * half, 16), 16))
        return carry

    lax.fori_loop(0, 2, step, 0)
    for block in range(4):
        leave(made_ref, output_ref, left, block).wait()


def backward_kernel(received_ref, slope_ref, depth_ref, point_ref, output_ref, made_ref, left):
    depth = depth_ref[...]
    point = spread_point(point_ref, 1)
    for half in range(2):
        rows = half_rows(received_ref, half)
        for g in range(2):
            first = 8 * half + 4 * g
            for e in range(2):
                spectral = synthesis(rows, g, e, depth)
                for h in range(2):
                    x = first + 2 * h + e
                    total = spectral[h * CY : (h + 1) * CY] + dot(point, slope_ref[:, x].reshape(CY, L))
                    made_ref[:, x] = total.reshape(C, G, L).astype(BF)
            leave(made_ref, output_ref, left, 2 * half + g).start()
    for block in range(4):
        leave(made_ref, output_ref, left, block).wait()


SMEM = pl.BlockSpec(memory_space=pltpu.SMEM)
NEAR = pl.BlockSpec(memory_space=pltpu.VMEM)
FAR = pl.BlockSpec(memory_space=pl.ANY)
FIELD = jax.ShapeDtypeStruct((C, G, G, L), BF)
HELD = pltpu.VMEM((C, G, G, L), BF)
FOUR = pltpu.SemaphoreType.DMA((4,))
BIG = jax.ShapeDtypeStruct((8, 2, 32, 2 * CY), BF)
SMALL = jax.ShapeDtypeStruct((G, 8, CY), BF)
MODES = jax.ShapeDtypeStruct((32, 256), F32)


def call(kernel, out_shape, in_specs=None, out_specs=None, scratch=(), flops=0, moved=0, room=16, grid=()):
    extra = {}
    if in_specs is not None:
        extra = {"in_specs": in_specs, "out_specs": out_specs}
    return pl.pallas_call(
        kernel,
        out_shape=out_shape,
        grid=grid,
        scratch_shapes=scratch,
        compiler_params=pltpu.CompilerParams(vmem_limit_bytes=room * MIB),
        cost_estimate=pl.CostEstimate(flops=int(flops), bytes_accessed=moved, transcendentals=0),
        **extra,
    )


def exchange_rows(packed):
    moved = lax.all_to_all(packed.reshape(G, 32, 2 * CY), "gx", 0, 0, tiled=True)
    return moved


def exchange_columns(packed):
    return lax.all_to_all(packed, "gy", 0, 0, tiled=True)


def shards(saturation, spectral_weight, pointwise_weight, pointwise_bias, cotangent):
    depth = jnp.asarray(depth_table(), BF)
    rows = jnp.asarray(row_matrix(), BF)
    rows_back = jnp.asarray(row_matrix().T, BF)
    columns = jnp.asarray(column_matrix(), BF)
    order = jnp.asarray(order_matrix(), BF)
    weight = jnp.transpose(spectral_weight, (1, 3, 4, 0, 2)).reshape(3, C, 2 * C, K)

    depth_call = call(
        depth_kernel,
        BIG,
        [pl.BlockSpec((C, 8, G, L), lambda n: (0, n, 0, 0)), pl.BlockSpec((64, L), lambda n: (0, 0))],
        pl.BlockSpec((8, 2, 16, 2 * CY), lambda n: (0, 0, n, 0)),
        flops=170e6,
        moved=3300000,
        room=60,
        grid=(2,),
    )
    row_call = call(row_kernel, SMALL, flops=170e6, moved=1000000)
    row_back_call = call(row_back_kernel, jax.ShapeDtypeStruct((G, 32, 2 * CY), BF), flops=170e6, moved=1000000)
    mix_scratch = [pltpu.VMEM((32, 256), F32), pltpu.VMEM((2 * C, 128), F32)]
    mix_call = call(mix_kernel, (SMALL, MODES), [NEAR] * 4, (NEAR, NEAR), mix_scratch, 200e6, 2500000)
    back_mix_call = call(
        back_mix_kernel,
        (SMALL, jax.ShapeDtypeStruct((3, C, 2 * C, K), F32)),
        [NEAR] * 5,
        (NEAR, NEAR),
        mix_scratch,
        200e6,
        4000000,
    )

    received = exchange_rows(depth_call(saturation, depth))
    received = exchange_columns(row_call(received, rows))
    sent, spectrum = mix_call(received, order, columns, weight)
    received = exchange_columns(sent)
    received = exchange_rows(row_back_call(received, rows_back))
    layer_output, slope, sent = call(
        forward_kernel,
        (FIELD, FIELD, BIG),
        [NEAR] * 5 + [SMEM],
        (FAR, NEAR, NEAR),
        [pltpu.VMEM((CY, CY), BF), HELD, FOUR],
        1500e6,
        12000000,
        20,
    )(received.reshape(BIG.shape), saturation, cotangent, depth, pointwise_weight, pointwise_bias)
    received = exchange_rows(sent)
    received = exchange_columns(row_call(received, rows))
    sent, gradient = back_mix_call(received, order, columns, weight, spectrum)
    received = exchange_columns(sent)
    received = exchange_rows(row_back_call(received, rows_back))
    input_gradient = call(
        backward_kernel,
        FIELD,
        [NEAR] * 4,
        FAR,
        [HELD, FOUR],
        1300e6,
        6000000,
        16,
    )(received.reshape(BIG.shape), slope, depth, pointwise_weight)
    gradient = jnp.transpose(gradient.reshape(3, C, C, 2, K), (3, 0, 4, 1, 2))
    return layer_output, input_gradient, gradient


def solution(mesh):
    return jax.shard_map(
        shards,
        mesh=mesh,
        in_specs=(
            P(None, "gx", "gy", None),
            P(None, ("gx", "gy"), None, None, None),
            P(),
            P(),
            P(None, "gx", "gy", None),
        ),
        out_specs=(
            P(None, "gx", "gy", None),
            P(None, "gx", "gy", None),
            P(None, ("gx", "gy"), None, None, None),
        ),
        check_vma=False,
    )
```

time: 171 us -> 165 us (0.965)
  blocking collectives: 54.1 us -> 145 us
  waiting for transfers between devices: 45.3 us -> 0 us
  starting transfers between devices: 26.4 us -> 0 us
  local copies, waits for them, and re-layouts: 18.4 us -> 0.06 us
  Pallas kernels: 21.9 us -> 18.6 us
  other arithmetic: 2.27 us -> 0 us
    all_to_all x1 -> x4, blocking collectives: 24.3 us -> 104 us  [exchange_rows(): lax.all_to_all(packed.reshape(G, 32, 2 * CY), 'gx', 0, 0, tiled=True)]
    all_to_all x4 -> x0, waiting for transfers between devices: 45.3 us -> none  [the longest x3 39.4 us: exchange_rows(): lax.all_to_all(packed.reshape(G, 32, 2 * CY), 'gx', 0, 0, tiled=True)]
    all_to_all x4 -> x0, starting transfers between devices: 26.4 us -> none  [the longest x3 18.9 us: exchange_rows(): lax.all_to_all(packed.reshape(G, 32, 2 * CY), 'gx', 0, 0, tiled=True)]
    all_to_all x3 -> x4, blocking collectives: 29.7 us -> 41.1 us  [exchange_columns(): return lax.all_to_all(packed, 'gy', 0, 0, tiled=True)]
    reshape x3 -> x0, local copies, waits for them, and re-layouts: 6.47 us -> none  [the longest x2 4.7 us: shards(): spectral_weight.reshape(2, 3 * K, C, C)]
    mul x2 -> x0, local copies, waits for them, and re-layouts: 6.3 us -> none  [the longest x1 3.47 us: shards(): point = jnp.kron(pointwise_weight.T, eye)]
    unnamed x19 -> x20, local copies, waits for them, and re-layouts: 4.43 us -> 0.06 us
    mul x1 -> x0, other arithmetic: 2.26 us -> none  [shards(): point_back = jnp.kron(pointwise_weight, eye)]
  transfers between devices with their start and end apart: 4 -> 0, of which waited for: 4 -> 0; matrix products, arithmetic and copies ran while one was open for 12% -> 0% of each run, Pallas kernels for 0% -> 0%
where the time goes in v3:
time: 165 us
  blocking collectives  145 us (88%)
  Pallas kernels  18.6 us (11%)
    all_to_all x4, blocking collectives, exchange_rows(): lax.all_to_all(packed.reshape(G, 32, 2 * CY), 'gx', 0, 0, tiled=True)  104 us
    all_to_all x4, blocking collectives, exchange_columns(): return lax.all_to_all(packed, 'gy', 0, 0, tiled=True)  41.1 us
    pallas_call x1, Pallas kernels, shards(): call(forward_kernel, (FIELD, FIELD, BIG), [NEAR] * 5 + [SMEM], (FAR, NEAR...  6.77 us

profile of v3, /device:TPU:1, one launch (start us, length us, event | category | flops | bytes accessed | tf_op | source)
XLA Modules:
  0.0 164.8 jit_solution(9176863501965037357)
XLA Ops:
  0.6 0.0 copy-start.6
  0.6 0.0 copy-start.2
  0.7 0.0 copy-start.4
  0.7 0.0 copy-start.1
  0.7 3.3 %shard_map.121 = bf16[8,2,32,640]{3,2,1,0:T(8,128)(2,1)} custom-call(bf16[20,16,16,256]{3,2,1,0:T(8,128)(2,1)} %volume_ref.3, bf16[64,256]{1,0:T(8,128)(2,1)} %constant.10.clone.depth_ref), custom_call_target="tpu_custom_call" | custom-call | flops 170000000 | bytes 3300000 | tf_op jit(solution)/shard_map/pallas_call | solution.py:343
  3.9 32.8 %all_to_all.40.received_ref = bf16[16,32,640]{2,1,0:T(8,128)(2,1)S(1)} all-to-all(bf16[16,32,640]{2,1,0:T(8,128)(2,1)} %bitcast.15), channel_id=1, replica_groups=mesh['gx'=16,'gy'=16] {'gx'}, dimensions={0} | all-to-all | bytes 1310720 | tf_op jit(solution)/shard_map/all_to_all | solution.py:303
  36.7 0.0 copy-done.6
  36.7 0.4 shard_map.122
  37.2 12.4 %all_to_all.41.received_ref = bf16[16,8,320]{2,1,0:T(8,128)(2,1)S(1)} all-to-all(bf16[16,8,320]{2,1,0:T(8,128)(2,1)S(1)} %shard_map.122), channel_id=1, replica_groups=mesh['gx'=16,'gy'=16] {'gy'}, dimensions={0} | all-to-all | bytes 163840 | tf_op jit(solution)/shard_map/all_to_all | solution.py:308
  49.6 0.0 copy-done.2
  49.6 0.0 copy-done.1
  49.6 0.0 copy-start
  49.6 0.0 copy-start.3
  49.6 0.0 copy-start.7
  49.6 0.0 copy-start.8
  49.6 0.0 copy-start.9
  49.6 1.3 shard_map.123
  50.9 9.0 %all_to_all.42.received_ref = bf16[16,8,320]{2,1,0:T(8,128)(2,1)S(1)} all-to-all(bf16[16,8,320]{2,1,0:T(8,128)(2,1)S(1)} %get-tuple-element.10), channel_id=1, replica_groups=mesh['gx'=16,'gy'=16] {'gy'}, dimensions={0} | all-to-all | bytes 163840 | tf_op jit(solution)/shard_map/all_to_all | solution.py:308
  59.9 0.4 shard_map.124
  60.3 23.8 %all_to_all.43 = bf16[16,32,640]{2,1,0:T(8,128)(2,1)S(1)} all-to-all(bf16[16,32,640]{2,1,0:T(8,128)(2,1)S(1)} %shard_map.124), channel_id=1, replica_groups=mesh['gx'=16,'gy'=16] {'gx'}, dimensions={0} | all-to-all | bytes 1310720 | tf_op jit(solution)/shard_map/all_to_all | solution.py:303
  84.1 0.0 copy-done.7
  84.1 0.0 copy-done.8
  84.1 0.0 copy-done.9
  84.1 6.8 %shard_map.125 = (bf16[20,16,16,256]{3,2,1,0:T(8,128)(2,1)}, bf16[20,16,16,256]{3,2,1,0:T(8,128)(2,1)S(1)}, bf16[8,2,32,640]{3,2,1,0:T(8,128)(2,1)S(1)}) custom-call(bf16[8,2,32,640]{3,2,1,0:T(8,128)(2,1)S(1)} %bitcast.12, bf16[20,16,16,256]{3,2,1,0:T(8,128)(2,1)S(1)} %copy-done, bf16[20,16,16,256]{3,2,1,0:T(8,128)(2,1)S(1)} %copy-done.3, ...), custom_call_target="tpu_custom_call" | custom-call | flops 1500000000 | bytes 12000000 | tf_op jit(solution)/shard_map/pallas_call | solution.py:348
  90.9 23.9 %all_to_all.44.received_ref = bf16[16,32,640]{2,1,0:T(8,128)(2,1)S(1)} all-to-all(bf16[16,32,640]{2,1,0:T(8,128)(2,1)S(1)} %bitcast.14), channel_id=1, replica_groups=mesh['gx'=16,'gy'=16] {'gx'}, dimensions={0} | all-to-all | bytes 1310720 | tf_op jit(solution)/shard_map/all_to_all | solution.py:303
  114.8 0.4 shard_map.126
  115.3 10.8 %all_to_all.45.received_ref = bf16[16,8,320]{2,1,0:T(8,128)(2,1)S(1)} all-to-all(bf16[16,8,320]{2,1,0:T(8,128)(2,1)S(1)} %shard_map.126), channel_id=1, replica_groups=mesh['gx'=16,'gy'=16] {'gy'}, dimensions={0} | all-to-all | bytes 163840 | tf_op jit(solution)/shard_map/all_to_all | solution.py:308
  126.1 2.4 %shard_map.127 = (bf16[16,8,320]{2,1,0:T(8,128)(2,1)S(1)}, f32[3,20,40,24]{3,2,1,0:T(8,128)}) custom-call(bf16[16,8,320]{2,1,0:T(8,128)(2,1)S(1)} %all_to_all.45.received_ref, bf16[512,320]{1,0:T(8,128)(2,1)S(1)} %copy-done.4, bf16[2048,256]{1,0:T(8,128)(2,1)S(1)} %copy-done.2, f32[3,20,40,24]{3,2,1,0:T(8,128)S(1)} %bitcast.11, ...), custom_call_target="tpu_custom_call" | custom-call | flops 200000000 | bytes 4000000 | tf_op jit(solution)/shard_map/pallas_call | solution.py:360
  128.5 8.9 %all_to_all.46.received_ref = bf16[16,8,320]{2,1,0:T(8,128)(2,1)S(1)} all-to-all(bf16[16,8,320]{2,1,0:T(8,128)(2,1)S(1)} %get-tuple-element.14), channel_id=1, replica_groups=mesh['gx'=16,'gy'=16] {'gy'}, dimensions={0} | all-to-all | bytes 163840 | tf_op jit(solution)/shard_map/all_to_all | solution.py:308
  137.4 0.4 shard_map.128
  137.7 23.8 %all_to_all.47 = bf16[16,32,640]{2,1,0:T(8,128)(2,1)S(1)} all-to-all(bf16[16,32,640]{2,1,0:T(8,128)(2,1)S(1)} %shard_map.128), channel_id=1, replica_groups=mesh['gx'=16,'gy'=16] {'gx'}, dimensions={0} | all-to-all | bytes 1310720 | tf_op jit(solution)/shard_map/all_to_all | solution.py:303
  161.5 3.2 %shard_map.129 = bf16[20,16,16,256]{3,2,1,0:T(8,128)(2,1)} custom-call(bf16[8,2,32,640]{3,2,1,0:T(8,128)(2,1)S(1)} %bitcast.13, bf16[20,16,16,256]{3,2,1,0:T(8,128)(2,1)S(1)} %get-tuple-element.15.slope_ref, bf16[64,256]{1,0:T(8,128)(2,1)S(1)} %copy-done.7, bf16[20,20]{1,0:T(8,128)(2,1)S(1)} %copy-done.8), custom_call_target="tpu_custom_call" | custom-call | flops 1300000000 | bytes 6000000 | tf_op jit(solution)/shard_map/pallas_call | solution.py:363
  (5 shorter events, 0.0 us)
Async XLA Ops:
  0.6 36.1 %copy-start.6 = (bf16[256,512]{1,0:T(8,128)(2,1)S(1)}, bf16[256,512]{1,0:T(8,128)(2,1)}, u32[]{:S(2)}) copy-start(bf16[256,512]{1,0:T(8,128)(2,1)} %constant.11.clone.matrix_ref) | copy-start | bytes 786436
  0.6 48.9 %copy-start.2 = (bf16[2048,256]{1,0:T(8,128)(2,1)S(1)}, bf16[2048,256]{1,0:T(8,128)(2,1)}, u32[]{:S(2)}) copy-start(bf16[2048,256]{1,0:T(8,128)(2,1)} %constant.13.clone.column_ref) | copy-start | bytes 3145732
  0.7 48.9 %copy-start.4 = (bf16[512,320]{1,0:T(8,128)(2,1)S(1)}, bf16[512,320]{1,0:T(8,128)(2,1)}, u32[]{:S(2)}) copy-start(bf16[512,320]{1,0:T(8,128)(2,1)} %constant.14.clone.order_ref) | copy-start | bytes 983044
  0.7 48.9 %copy-start.1 = (f32[2,3,24,20,20]{2,0,4,3,1:T(2,128)S(1)}, f32[2,3,24,20,20]{2,0,4,3,1:T(2,128)}, u32[]{:S(2)}) copy-start(f32[2,3,24,20,20]{2,0,4,3,1:T(2,128)} %param.11) | copy-start | bytes 691204
  3.9 56.0 %copy-start.5 = (bf16[512,256]{1,0:T(8,128)(2,1)S(1)}, bf16[512,256]{1,0:T(8,128)(2,1)}, u32[]{:S(2)}) copy-start(bf16[512,256]{1,0:T(8,128)(2,1)} %constant.12.clone.matrix_ref) | copy-start | bytes 786436
  49.6 34.5 %copy-start = (bf16[20,16,16,256]{3,2,1,0:T(8,128)(2,1)S(1)}, bf16[20,16,16,256]{3,2,1,0:T(8,128)(2,1)}, u32[]{:S(2)}) copy-start(bf16[20,16,16,256]{3,2,1,0:T(8,128)(2,1)} %volume_ref.3) | copy-start | bytes 7864324
  49.6 34.5 %copy-start.3 = (bf16[20,16,16,256]{3,2,1,0:T(8,128)(2,1)S(1)}, bf16[20,16,16,256]{3,2,1,0:T(8,128)(2,1)}, u32[]{:S(2)}) copy-start(bf16[20,16,16,256]{3,2,1,0:T(8,128)(2,1)} %cotangent_ref.1) | copy-start | bytes 7864324
  49.6 34.5 %copy-start.7 = (bf16[64,256]{1,0:T(8,128)(2,1)S(1)}, bf16[64,256]{1,0:T(8,128)(2,1)}, u32[]{:S(2)}) copy-start(bf16[64,256]{1,0:T(8,128)(2,1)} %constant.10.clone.depth_ref) | copy-start | bytes 98308
  49.6 34.5 %copy-start.8 = (bf16[20,20]{1,0:T(8,128)(2,1)S(1)}, bf16[20,20]{1,0:T(8,128)(2,1)}, u32[]{:S(2)}) copy-start(bf16[20,20]{1,0:T(8,128)(2,1)} %point_ref.3) | copy-start | bytes 2404
  49.6 34.5 %copy-start.9 = (f32[20]{0:T(128)S(1)}, f32[20]{0:T(128)}, u32[]{:S(2)}) copy-start(f32[20]{0:T(128)} %bias_ref.1) | copy-start | bytes 244

commit v4 on v3

--- a/solution.py
+++ b/solution.py
@@ -95,6 +95,26 @@
 def send_planes(tiles, send_ref, rows):
     for parity in range(2):
         send_ref[:, parity, rows] = jnp.concatenate([tiles[0][parity], tiles[1][parity]], 1).astype(BF)
+
+
+def left_rows(even, odd, e):
+    low = lax.broadcasted_iota(jnp.int32, even.shape, 1) < 4
+    if e == 0:
+        both = jnp.where(low, even, pltpu.roll(odd, 4, 1))
+    else:
+        both = jnp.where(low, pltpu.roll(even, 4, 1), odd)
+    return both.reshape(64, 2 * CY).T.astype(BF)
+
+
+def full_planes(rows, g, e, depth, point, plane):
+    left = left_rows(rows[:, 0, 8 * g : 8 * g + 8], rows[:, 1, 8 * g : 8 * g + 8], e)
+    return [
+        dot(
+            jnp.concatenate([point, left[h * CY : (h + 1) * CY]], 1),
+            jnp.concatenate([plane(2 * h + e), depth], 0),
+        )
+        for h in range(2)
+    ]
 
 
 def synthesis(rows, g, e, depth):
@@ -198,7 +218,7 @@
 
 def activation(pre):
     cumulative = 0.5 + 0.5 * lax.erf(pre * (1.0 / math.sqrt(2.0)))
-    density = jnp.exp(-0.5 * pre * pre) * (1.0 / math.sqrt(2.0 * math.pi))
+    density = jnp.exp2(pre * pre * (-0.5 / math.log(2.0))) * (1.0 / math.sqrt(2.0 * math.pi))
     return cumulative, density
 
 
@@ -235,10 +255,10 @@
         for g in range(2):
             first = 8 * half + 4 * g
             for e in range(2):
-                spectral = synthesis(rows, g, e, depth)
+                totals = full_planes(rows, g, e, depth, point, lambda k: volume_ref[:, first + k].reshape(CY, L))
                 for h in range(2):
                     x = first + 2 * h + e
-                    total = spectral[h * CY : (h + 1) * CY] + dot(point, volume_ref[:, x].reshape(CY, L))
+                    total = totals[h]
                     for c in range(C):
                         pre = total[c * G : (c + 1) * G] + bias_ref[c]
                         cumulative, density = activation(pre)

time: 165 us -> 164 us (level)
  no operation moved by 1% of the time
where the time goes in v4:
time: 164 us
  blocking collectives  145 us (88%)
  Pallas kernels  17.8 us (11%)
    all_to_all x4, blocking collectives, exchange_rows(): lax.all_to_all(packed.reshape(G, 32, 2 * CY), 'gx', 0, 0, tiled=True)  104 us
    all_to_all x4, blocking collectives, exchange_columns(): return lax.all_to_all(packed, 'gy', 0, 0, tiled=True)  41.1 us
    pallas_call x1, Pallas kernels, shards(): call(forward_kernel, (FIELD, FIELD, BIG), [NEAR] * 5 + [SMEM], (FAR, NEAR...  6.02 us

profile of v4, /device:TPU:1, one launch (start us, length us, event | category | flops | bytes accessed | tf_op | source)
XLA Modules:
  0.0 164.0 jit_solution(11784282385778211548)
XLA Ops:
  0.6 0.0 copy-start.6
  0.6 0.0 copy-start.2
  0.7 0.0 copy-start.4
  0.7 0.0 copy-start.1
  0.7 3.3 %shard_map.121 = bf16[8,2,32,640]{3,2,1,0:T(8,128)(2,1)} custom-call(bf16[20,16,16,256]{3,2,1,0:T(8,128)(2,1)} %volume_ref.3, bf16[64,256]{1,0:T(8,128)(2,1)} %constant.10.clone.depth_ref), custom_call_target="tpu_custom_call" | custom-call | flops 170000000 | bytes 3300000 | tf_op jit(solution)/shard_map/pallas_call | solution.py:363
  3.9 32.8 %all_to_all.40.received_ref = bf16[16,32,640]{2,1,0:T(8,128)(2,1)S(1)} all-to-all(bf16[16,32,640]{2,1,0:T(8,128)(2,1)} %bitcast.15), channel_id=1, replica_groups=mesh['gx'=16,'gy'=16] {'gx'}, dimensions={0} | all-to-all | bytes 1310720 | tf_op jit(solution)/shard_map/all_to_all | solution.py:323
  36.7 0.0 copy-done.6
  36.7 0.4 shard_map.122
  37.2 12.4 %all_to_all.41.received_ref = bf16[16,8,320]{2,1,0:T(8,128)(2,1)S(1)} all-to-all(bf16[16,8,320]{2,1,0:T(8,128)(2,1)S(1)} %shard_map.122), channel_id=1, replica_groups=mesh['gx'=16,'gy'=16] {'gy'}, dimensions={0} | all-to-all | bytes 163840 | tf_op jit(solution)/shard_map/all_to_all | solution.py:328
  49.6 0.0 copy-done.2
  49.6 0.0 copy-done.1
  49.6 0.0 copy-start
  49.6 0.0 copy-start.3
  49.6 0.0 copy-start.7
  49.6 0.0 copy-start.8
  49.6 0.0 copy-start.9
  49.6 1.3 shard_map.123
  50.9 9.0 %all_to_all.42.received_ref = bf16[16,8,320]{2,1,0:T(8,128)(2,1)S(1)} all-to-all(bf16[16,8,320]{2,1,0:T(8,128)(2,1)S(1)} %get-tuple-element.10), channel_id=1, replica_groups=mesh['gx'=16,'gy'=16] {'gy'}, dimensions={0} | all-to-all | bytes 163840 | tf_op jit(solution)/shard_map/all_to_all | solution.py:328
  59.9 0.4 shard_map.124
  60.3 23.8 %all_to_all.43 = bf16[16,32,640]{2,1,0:T(8,128)(2,1)S(1)} all-to-all(bf16[16,32,640]{2,1,0:T(8,128)(2,1)S(1)} %shard_map.124), channel_id=1, replica_groups=mesh['gx'=16,'gy'=16] {'gx'}, dimensions={0} | all-to-all | bytes 1310720 | tf_op jit(solution)/shard_map/all_to_all | solution.py:323
  84.1 0.0 copy-done.7
  84.1 0.0 copy-done.8
  84.1 0.0 copy-done.9
  84.1 6.0 %shard_map.125 = (bf16[20,16,16,256]{3,2,1,0:T(8,128)(2,1)}, bf16[20,16,16,256]{3,2,1,0:T(8,128)(2,1)S(1)}, bf16[8,2,32,640]{3,2,1,0:T(8,128)(2,1)S(1)}) custom-call(bf16[8,2,32,640]{3,2,1,0:T(8,128)(2,1)S(1)} %bitcast.12, bf16[20,16,16,256]{3,2,1,0:T(8,128)(2,1)S(1)} %copy-done, bf16[20,16,16,256]{3,2,1,0:T(8,128)(2,1)S(1)} %copy-done.3, ...), custom_call_target="tpu_custom_call" | custom-call | flops 1500000000 | bytes 12000000 | tf_op jit(solution)/shard_map/pallas_call | solution.py:368
  90.2 23.9 %all_to_all.44.received_ref = bf16[16,32,640]{2,1,0:T(8,128)(2,1)S(1)} all-to-all(bf16[16,32,640]{2,1,0:T(8,128)(2,1)S(1)} %bitcast.14), channel_id=1, replica_groups=mesh['gx'=16,'gy'=16] {'gx'}, dimensions={0} | all-to-all | bytes 1310720 | tf_op jit(solution)/shard_map/all_to_all | solution.py:323
  114.1 0.4 shard_map.126
  114.5 10.8 %all_to_all.45.received_ref = bf16[16,8,320]{2,1,0:T(8,128)(2,1)S(1)} all-to-all(bf16[16,8,320]{2,1,0:T(8,128)(2,1)S(1)} %shard_map.126), channel_id=1, replica_groups=mesh['gx'=16,'gy'=16] {'gy'}, dimensions={0} | all-to-all | bytes 163840 | tf_op jit(solution)/shard_map/all_to_all | solution.py:328
  125.4 2.4 %shard_map.127 = (bf16[16,8,320]{2,1,0:T(8,128)(2,1)S(1)}, f32[3,20,40,24]{3,2,1,0:T(8,128)}) custom-call(bf16[16,8,320]{2,1,0:T(8,128)(2,1)S(1)} %all_to_all.45.received_ref, bf16[512,320]{1,0:T(8,128)(2,1)S(1)} %copy-done.4, bf16[2048,256]{1,0:T(8,128)(2,1)S(1)} %copy-done.2, f32[3,20,40,24]{3,2,1,0:T(8,128)S(1)} %bitcast.11, ...), custom_call_target="tpu_custom_call" | custom-call | flops 200000000 | bytes 4000000 | tf_op jit(solution)/shard_map/pallas_call | solution.py:380
  127.8 8.9 %all_to_all.46.received_ref = bf16[16,8,320]{2,1,0:T(8,128)(2,1)S(1)} all-to-all(bf16[16,8,320]{2,1,0:T(8,128)(2,1)S(1)} %get-tuple-element.14), channel_id=1, replica_groups=mesh['gx'=16,'gy'=16] {'gy'}, dimensions={0} | all-to-all | bytes 163840 | tf_op jit(solution)/shard_map/all_to_all | solution.py:328
  136.6 0.4 shard_map.128
  137.0 23.8 %all_to_all.47 = bf16[16,32,640]{2,1,0:T(8,128)(2,1)S(1)} all-to-all(bf16[16,32,640]{2,1,0:T(8,128)(2,1)S(1)} %shard_map.128), channel_id=1, replica_groups=mesh['gx'=16,'gy'=16] {'gx'}, dimensions={0} | all-to-all | bytes 1310720 | tf_op jit(solution)/shard_map/all_to_all | solution.py:323
  160.8 3.2 %shard_map.129 = bf16[20,16,16,256]{3,2,1,0:T(8,128)(2,1)} custom-call(bf16[8,2,32,640]{3,2,1,0:T(8,128)(2,1)S(1)} %bitcast.13, bf16[20,16,16,256]{3,2,1,0:T(8,128)(2,1)S(1)} %get-tuple-element.15.slope_ref, bf16[64,256]{1,0:T(8,128)(2,1)S(1)} %copy-done.7, bf16[20,20]{1,0:T(8,128)(2,1)S(1)} %copy-done.8), custom_call_target="tpu_custom_call" | custom-call | flops 1300000000 | bytes 6000000 | tf_op jit(solution)/shard_map/pallas_call | solution.py:383
  (5 shorter events, 0.0 us)
Async XLA Ops:
  0.6 36.1 %copy-start.6 = (bf16[256,512]{1,0:T(8,128)(2,1)S(1)}, bf16[256,512]{1,0:T(8,128)(2,1)}, u32[]{:S(2)}) copy-start(bf16[256,512]{1,0:T(8,128)(2,1)} %constant.11.clone.matrix_ref) | copy-start | bytes 786436
  0.6 48.9 %copy-start.2 = (bf16[2048,256]{1,0:T(8,128)(2,1)S(1)}, bf16[2048,256]{1,0:T(8,128)(2,1)}, u32[]{:S(2)}) copy-start(bf16[2048,256]{1,0:T(8,128)(2,1)} %constant.13.clone.column_ref) | copy-start | bytes 3145732
  0.7 48.9 %copy-start.4 = (bf16[512,320]{1,0:T(8,128)(2,1)S(1)}, bf16[512,320]{1,0:T(8,128)(2,1)}, u32[]{:S(2)}) copy-start(bf16[512,320]{1,0:T(8,128)(2,1)} %constant.14.clone.order_ref) | copy-start | bytes 983044
  0.7 48.9 %copy-start.1 = (f32[2,3,24,20,20]{2,0,4,3,1:T(2,128)S(1)}, f32[2,3,24,20,20]{2,0,4,3,1:T(2,128)}, u32[]{:S(2)}) copy-start(f32[2,3,24,20,20]{2,0,4,3,1:T(2,128)} %param.11) | copy-start | bytes 691204
  3.9 56.0 %copy-start.5 = (bf16[512,256]{1,0:T(8,128)(2,1)S(1)}, bf16[512,256]{1,0:T(8,128)(2,1)}, u32[]{:S(2)}) copy-start(bf16[512,256]{1,0:T(8,128)(2,1)} %constant.12.clone.matrix_ref) | copy-start | bytes 786436
  49.6 34.5 %copy-start = (bf16[20,16,16,256]{3,2,1,0:T(8,128)(2,1)S(1)}, bf16[20,16,16,256]{3,2,1,0:T(8,128)(2,1)}, u32[]{:S(2)}) copy-start(bf16[20,16,16,256]{3,2,1,0:T(8,128)(2,1)} %volume_ref.3) | copy-start | bytes 7864324
  49.6 34.5 %copy-start.3 = (bf16[20,16,16,256]{3,2,1,0:T(8,128)(2,1)S(1)}, bf16[20,16,16,256]{3,2,1,0:T(8,128)(2,1)}, u32[]{:S(2)}) copy-start(bf16[20,16,16,256]{3,2,1,0:T(8,128)(2,1)} %cotangent_ref.1) | copy-start | bytes 7864324
  49.6 34.5 %copy-start.7 = (bf16[64,256]{1,0:T(8,128)(2,1)S(1)}, bf16[64,256]{1,0:T(8,128)(2,1)}, u32[]{:S(2)}) copy-start(bf16[64,256]{1,0:T(8,128)(2,1)} %constant.10.clone.depth_ref) | copy-start | bytes 98308
  49.6 34.5 %copy-start.8 = (bf16[20,20]{1,0:T(8,128)(2,1)S(1)}, bf16[20,20]{1,0:T(8,128)(2,1)}, u32[]{:S(2)}) copy-start(bf16[20,20]{1,0:T(8,128)(2,1)} %point_ref.3) | copy-start | bytes 2404
  49.6 34.5 %copy-start.9 = (f32[20]{0:T(128)S(1)}, f32[20]{0:T(128)}, u32[]{:S(2)}) copy-start(f32[20]{0:T(128)} %bias_ref.1) | copy-start | bytes 244

commit v5 on v4

--- a/solution.py
+++ b/solution.py
@@ -177,13 +177,14 @@
 
 
 def mix_kernel(
-    received_ref, order_ref, column_ref, weight_ref, send_ref, spectrum_ref, mixed_ref, parts_ref
+    received_ref, order_ref, column_ref, weight_ref, send_ref, spectrum_ref, wide_ref, mixed_ref, parts_ref
 ):
     spectrum_ref[...] = column_analysis(received_ref, order_ref, column_ref)
     by_real = jnp.zeros((2 * C, 128), F32)
     by_imag = jnp.zeros((2 * C, 128), F32)
     for i in range(C):
         weight = weight_rows(weight_ref, i)
+        wide_ref[i] = weight
         by_real += weight * spectrum_ref[i : i + 1, :128]
         by_imag += weight * spectrum_ref[i : i + 1, 128:]
     is_real, other = partner(by_imag)
@@ -206,7 +207,7 @@
     turned = jnp.where(is_real, other, -other)
     mixed_ref[...] = jnp.zeros((32, 256), F32)
     for i in range(C):
-        weight = weight_rows(weight_ref, i)
+        weight = weight_ref[i]
         mixed_ref[i : i + 1, :128] = jnp.sum(weight * upstream, 0, keepdims=True)
         mixed_ref[i : i + 1, 128:] = jnp.sum(weight * turned, 0, keepdims=True)
     column_synthesis(mixed_ref[...], order_ref, column_ref, send_ref)
@@ -349,7 +350,8 @@
     row_call = call(row_kernel, SMALL, flops=170e6, moved=1000000)
     row_back_call = call(row_back_kernel, jax.ShapeDtypeStruct((G, 32, 2 * CY), BF), flops=170e6, moved=1000000)
     mix_scratch = [pltpu.VMEM((32, 256), F32), pltpu.VMEM((2 * C, 128), F32)]
-    mix_call = call(mix_kernel, (SMALL, MODES), [NEAR] * 4, (NEAR, NEAR), mix_scratch, 200e6, 2500000)
+    wide = jax.ShapeDtypeStruct((C, 2 * C, 128), F32)
+    mix_call = call(mix_kernel, (SMALL, MODES, wide), [NEAR] * 4, (NEAR,) * 3, mix_scratch, 200e6, 2500000)
     back_mix_call = call(
         back_mix_kernel,
         (SMALL, jax.ShapeDtypeStruct((3, C, 2 * C, K), F32)),
@@ -362,7 +364,7 @@
 
     received = exchange_rows(depth_call(saturation, depth))
     received = exchange_columns(row_call(received, rows))
-    sent, spectrum = mix_call(received, order, columns, weight)
+    sent, spectrum, weight = mix_call(received, order, columns, weight)
     received = exchange_columns(sent)
     received = exchange_rows(row_back_call(received, rows_back))
     layer_output, slope, sent = call(

time: 164 us -> 164 us (level)
  no operation moved by 1% of the time
where the time goes in v5:
time: 164 us
  blocking collectives  145 us (88%)
  Pallas kernels  17.8 us (11%)
    all_to_all x4, blocking collectives, exchange_rows(): lax.all_to_all(packed.reshape(G, 32, 2 * CY), 'gx', 0, 0, tiled=True)  104 us
    all_to_all x4, blocking collectives, exchange_columns(): return lax.all_to_all(packed, 'gy', 0, 0, tiled=True)  41.1 us
    pallas_call x1, Pallas kernels, shards(): call(forward_kernel, (FIELD, FIELD, BIG), [NEAR] * 5 + [SMEM], (FAR, NEAR...  6.02 us

profile of v5, /device:TPU:1, one launch (start us, length us, event | category | flops | bytes accessed | tf_op | source)
XLA Modules:
  0.0 164.1 jit_solution(4991559989389445556)
XLA Ops:
  0.6 0.0 copy-start.6
  0.6 0.0 copy-start.1
  0.7 0.0 copy-start.3
  0.7 0.0 copy-start.4
  0.7 3.3 %shard_map.121 = bf16[8,2,32,640]{3,2,1,0:T(8,128)(2,1)} custom-call(bf16[20,16,16,256]{3,2,1,0:T(8,128)(2,1)} %volume_ref.3, bf16[64,256]{1,0:T(8,128)(2,1)} %constant.10.clone.depth_ref), custom_call_target="tpu_custom_call" | custom-call | flops 170000000 | bytes 3300000 | tf_op jit(solution)/shard_map/pallas_call | solution.py:365
  3.9 32.8 %all_to_all.40.received_ref = bf16[16,32,640]{2,1,0:T(8,128)(2,1)S(1)} all-to-all(bf16[16,32,640]{2,1,0:T(8,128)(2,1)} %bitcast.14), channel_id=1, replica_groups=mesh['gx'=16,'gy'=16] {'gx'}, dimensions={0} | all-to-all | bytes 1310720 | tf_op jit(solution)/shard_map/all_to_all | solution.py:324
  36.7 0.0 copy-done.6
  36.7 0.4 shard_map.122
  37.2 12.4 %all_to_all.41.received_ref = bf16[16,8,320]{2,1,0:T(8,128)(2,1)S(1)} all-to-all(bf16[16,8,320]{2,1,0:T(8,128)(2,1)S(1)} %shard_map.122), channel_id=1, replica_groups=mesh['gx'=16,'gy'=16] {'gy'}, dimensions={0} | all-to-all | bytes 163840 | tf_op jit(solution)/shard_map/all_to_all | solution.py:329
  49.6 0.0 copy-done.1
  49.6 0.0 copy-done.3
  49.6 0.0 copy-done.4
  49.6 0.0 copy-start
  49.6 0.0 copy-start.2
  49.6 0.0 copy-start.7
  49.6 0.0 copy-start.8
  49.6 0.0 copy-start.9
  49.6 1.3 shard_map.123
  50.9 9.0 %all_to_all.42.received_ref = bf16[16,8,320]{2,1,0:T(8,128)(2,1)S(1)} all-to-all(bf16[16,8,320]{2,1,0:T(8,128)(2,1)S(1)} %get-tuple-element.11), channel_id=1, replica_groups=mesh['gx'=16,'gy'=16] {'gy'}, dimensions={0} | all-to-all | bytes 163840 | tf_op jit(solution)/shard_map/all_to_all | solution.py:329
  59.9 0.0 copy-done.5
  59.9 0.4 shard_map.124
  60.3 23.8 %all_to_all.43 = bf16[16,32,640]{2,1,0:T(8,128)(2,1)S(1)} all-to-all(bf16[16,32,640]{2,1,0:T(8,128)(2,1)S(1)} %shard_map.124), channel_id=1, replica_groups=mesh['gx'=16,'gy'=16] {'gx'}, dimensions={0} | all-to-all | bytes 1310720 | tf_op jit(solution)/shard_map/all_to_all | solution.py:324
  84.1 0.0 copy-done
  84.1 6.0 %shard_map.125 = (bf16[20,16,16,256]{3,2,1,0:T(8,128)(2,1)}, bf16[20,16,16,256]{3,2,1,0:T(8,128)(2,1)S(1)}, bf16[8,2,32,640]{3,2,1,0:T(8,128)(2,1)S(1)}) custom-call(bf16[8,2,32,640]{3,2,1,0:T(8,128)(2,1)S(1)} %bitcast.10, bf16[20,16,16,256]{3,2,1,0:T(8,128)(2,1)S(1)} %copy-done, bf16[20,16,16,256]{3,2,1,0:T(8,128)(2,1)S(1)} %copy-done.2, ...), custom_call_target="tpu_custom_call" | custom-call | flops 1500000000 | bytes 12000000 | tf_op jit(solution)/shard_map/pallas_call | solution.py:370
  90.2 23.9 %all_to_all.44.received_ref = bf16[16,32,640]{2,1,0:T(8,128)(2,1)S(1)} all-to-all(bf16[16,32,640]{2,1,0:T(8,128)(2,1)S(1)} %bitcast.13), channel_id=1, replica_groups=mesh['gx'=16,'gy'=16] {'gx'}, dimensions={0} | all-to-all | bytes 1310720 | tf_op jit(solution)/shard_map/all_to_all | solution.py:324
  114.1 0.4 shard_map.126
  114.5 10.8 %all_to_all.45.received_ref = bf16[16,8,320]{2,1,0:T(8,128)(2,1)S(1)} all-to-all(bf16[16,8,320]{2,1,0:T(8,128)(2,1)S(1)} %shard_map.126), channel_id=1, replica_groups=mesh['gx'=16,'gy'=16] {'gy'}, dimensions={0} | all-to-all | bytes 163840 | tf_op jit(solution)/shard_map/all_to_all | solution.py:329
  125.3 2.4 %shard_map.127 = (bf16[16,8,320]{2,1,0:T(8,128)(2,1)S(1)}, f32[3,20,40,24]{3,2,1,0:T(8,128)}) custom-call(bf16[16,8,320]{2,1,0:T(8,128)(2,1)S(1)} %all_to_all.45.received_ref, bf16[512,320]{1,0:T(8,128)(2,1)S(1)} %copy-done.3, bf16[2048,256]{1,0:T(8,128)(2,1)S(1)} %copy-done.1, f32[20,40,128]{2,1,0:T(8,128)S(1)} %get-tuple-element.14.weight_ref, ...), custom_call_target="tpu_custom_call" | custom-call | flops 200000000 | bytes 4000000 | tf_op jit(solution)/shard_map/pallas_call | solution.py:382
  127.8 8.9 %all_to_all.46.received_ref = bf16[16,8,320]{2,1,0:T(8,128)(2,1)S(1)} all-to-all(bf16[16,8,320]{2,1,0:T(8,128)(2,1)S(1)} %get-tuple-element.16), channel_id=1, replica_groups=mesh['gx'=16,'gy'=16] {'gy'}, dimensions={0} | all-to-all | bytes 163840 | tf_op jit(solution)/shard_map/all_to_all | solution.py:329
  136.6 0.4 shard_map.128
  137.0 23.8 %all_to_all.47 = bf16[16,32,640]{2,1,0:T(8,128)(2,1)S(1)} all-to-all(bf16[16,32,640]{2,1,0:T(8,128)(2,1)S(1)} %shard_map.128), channel_id=1, replica_groups=mesh['gx'=16,'gy'=16] {'gx'}, dimensions={0} | all-to-all | bytes 1310720 | tf_op jit(solution)/shard_map/all_to_all | solution.py:324
  160.8 3.2 %shard_map.129 = bf16[20,16,16,256]{3,2,1,0:T(8,128)(2,1)} custom-call(bf16[8,2,32,640]{3,2,1,0:T(8,128)(2,1)S(1)} %bitcast.11, bf16[20,16,16,256]{3,2,1,0:T(8,128)(2,1)S(1)} %get-tuple-element.17.slope_ref, bf16[64,256]{1,0:T(8,128)(2,1)S(1)} %copy-done.7, bf16[20,20]{1,0:T(8,128)(2,1)S(1)} %copy-done.8), custom_call_target="tpu_custom_call" | custom-call | flops 1300000000 | bytes 6000000 | tf_op jit(solution)/shard_map/pallas_call | solution.py:385
  (5 shorter events, 0.0 us)
Async XLA Ops:
  0.6 36.1 %copy-start.6 = (bf16[256,512]{1,0:T(8,128)(2,1)S(1)}, bf16[256,512]{1,0:T(8,128)(2,1)}, u32[]{:S(2)}) copy-start(bf16[256,512]{1,0:T(8,128)(2,1)} %constant.11.clone.matrix_ref) | copy-start | bytes 786436
  0.6 48.9 %copy-start.1 = (bf16[2048,256]{1,0:T(8,128)(2,1)S(1)}, bf16[2048,256]{1,0:T(8,128)(2,1)}, u32[]{:S(2)}) copy-start(bf16[2048,256]{1,0:T(8,128)(2,1)} %constant.13.clone.column_ref) | copy-start | bytes 3145732
  0.7 48.9 %copy-start.3 = (bf16[512,320]{1,0:T(8,128)(2,1)S(1)}, bf16[512,320]{1,0:T(8,128)(2,1)}, u32[]{:S(2)}) copy-start(bf16[512,320]{1,0:T(8,128)(2,1)} %constant.14.clone.order_ref) | copy-start | bytes 983044
  0.7 48.9 %copy-start.4 = (f32[2,3,24,20,20]{2,0,4,3,1:T(2,128)S(1)}, f32[2,3,24,20,20]{2,0,4,3,1:T(2,128)}, u32[]{:S(2)}) copy-start(f32[2,3,24,20,20]{2,0,4,3,1:T(2,128)} %param.11) | copy-start | bytes 691204
  3.9 56.0 %copy-start.5 = (bf16[512,256]{1,0:T(8,128)(2,1)S(1)}, bf16[512,256]{1,0:T(8,128)(2,1)}, u32[]{:S(2)}) copy-start(bf16[512,256]{1,0:T(8,128)(2,1)} %constant.12.clone.matrix_ref) | copy-start | bytes 786436
  49.6 34.5 %copy-start = (bf16[20,16,16,256]{3,2,1,0:T(8,128)(2,1)S(1)}, bf16[20,16,16,256]{3,2,1,0:T(8,128)(2,1)}, u32[]{:S(2)}) copy-start(bf16[20,16,16,256]{3,2,1,0:T(8,128)(2,1)} %volume_ref.3) | copy-start | bytes 7864324
  49.6 34.5 %copy-start.2 = (bf16[20,16,16,256]{3,2,1,0:T(8,128)(2,1)S(1)}, bf16[20,16,16,256]{3,2,1,0:T(8,128)(2,1)}, u32[]{:S(2)}) copy-start(bf16[20,16,16,256]{3,2,1,0:T(8,128)(2,1)} %cotangent_ref.1) | copy-start | bytes 7864324
  49.6 34.5 %copy-start.7 = (bf16[64,256]{1,0:T(8,128)(2,1)S(1)}, bf16[64,256]{1,0:T(8,128)(2,1)}, u32[]{:S(2)}) copy-start(bf16[64,256]{1,0:T(8,128)(2,1)} %constant.10.clone.depth_ref) | copy-start | bytes 98308
  49.6 34.5 %copy-start.8 = (bf16[20,20]{1,0:T(8,128)(2,1)S(1)}, bf16[20,20]{1,0:T(8,128)(2,1)}, u32[]{:S(2)}) copy-start(bf16[20,20]{1,0:T(8,128)(2,1)} %point_ref.3) | copy-start | bytes 2404
  49.6 34.5 %copy-start.9 = (f32[20]{0:T(128)S(1)}, f32[20]{0:T(128)}, u32[]{:S(2)}) copy-start(f32[20]{0:T(128)} %bias_ref.1) | copy-start | bytes 244
